TPU v7x, 32 devices: a whole 2x2x4 slice. The times are simulated.
32 devices in a mesh: layer: 4 (over y, x), tx: 2 (over core), ty: 4 (over z).
Axes of the slice: x: 2, y: 2, z: 4, core: 2. Of those that a mesh axis runs over, the one named last changes fastest.
Arguments:
- shunt_conductance: float32 [4, 64, 512], P('layer', 'tx', 'ty'), may hold values from 0.02 to 2
- agg_map: int32 [4, 64, 512], P('layer', 'tx', 'ty'), may hold values from 0 to 127, as said below
- slot_current: float32 [4, 2, 4, 8, 128], P('layer', 'tx', 'ty'), may hold values from -12 to 12
- slot_node: int32 [4, 2, 4, 8, 128], P('layer', 'tx', 'ty'), may hold values from 0 to 4095
- slot_count: int32 [4, 2, 4, 8], P('layer', 'tx', 'ty'), may hold values from 16 to 128, as said below
Outputs:
- voltage_drop: float32 [4, 64, 512], P('layer', 'tx', 'ty')
- residual: float32 [4, 64, 512], P('layer', 'tx', 'ty')
Inputs may be any that keep to these rules, and one draw needn't show every extreme that they name: `slot_count`: live slots in each block from one source tile to one destination tile, at least 16; slots past them are padding, and at least one block is full. `agg_map`: coarse cell numbered row-major over the 8 x 16 coarse cells of the node's own die tile.
All inputs are finite; a program needn't handle non-finite values.
Results may differ from a plain program's by a relative error of at most 0.0003.
Values sent between devices are 32-bit elements; how exact they have to be, the bound alone decides.
A program may use at most 64 MiB of HBM per device.

v0:
```python
import jax
import jax.numpy as jnp
from jax import lax
from jax.sharding import PartitionSpec as P

CGX = 8
CGY = 16
ITERS = 3
SWEEPS = 3


VIA_CONDUCTANCE = 0.5
COARSE_EDGE = 8.0
RELAXATION = 0.6


def with_halo(block, sides, width):
    for axis, dim in sides:
        count = lax.axis_size(axis)
        forward = [(i, i + 1) for i in range(count - 1)]
        backward = [(target, source) for source, target in forward]
        low = lax.ppermute(
            lax.slice_in_dim(block, block.shape[dim] - width, None, axis=dim), axis, forward
        )
        high = lax.ppermute(lax.slice_in_dim(block, 0, width, axis=dim), axis, backward)
        block = jnp.concatenate([low, block, high], axis=dim)
    return block


def operate(source_field, diagonal):
    padded = with_halo(source_field, (("layer", 0), ("tx", 1), ("ty", 2)), 1)
    lateral = (
        padded[1:-1, 2:, 1:-1]
        + padded[1:-1, :-2, 1:-1]
        + padded[1:-1, 1:-1, 2:]
        + padded[1:-1, 1:-1, :-2]
    )
    vertical = padded[2:, 1:-1, 1:-1] + padded[:-2, 1:-1, 1:-1]
    return diagonal * source_field - lateral - VIA_CONDUCTANCE * vertical


def coarse_sweep(potential, coarse_rhs, coarse_diag, padded):
    beside = (
        padded[..., 2:, 1:-1]
        + padded[..., :-2, 1:-1]
        + padded[..., 1:-1, 2:]
        + padded[..., 1:-1, :-2]
    )
    return (
        potential
        + RELAXATION * (coarse_rhs - (coarse_diag * potential - COARSE_EDGE * beside)) / coarse_diag
    )


def restrict_layer(pair):
    source_field = pair[0]
    labels_all = pair[1]
    height = source_field.shape[0]
    breadth = source_field.shape[1]
    values = source_field.reshape(height // 8, 8 * breadth)
    labels_in = labels_all.reshape(height // 8, 8 * breadth)
    labels = jnp.arange(CGX * CGY, dtype=jnp.int32)

    def accumulate(running, block_pair):
        onehot = (block_pair[1][:, None] == labels[None, :]).astype(jnp.float32)
        added = jnp.dot(
            block_pair[0],
            onehot,
            precision=lax.Precision.HIGHEST,
            preferred_element_type=jnp.float32,
        )
        return (running + added, None)

    running, unused = lax.scan(
        accumulate, jnp.zeros((CGX * CGY,), jnp.float32), (values, labels_in)
    )
    return running.reshape(CGX, CGY)


def restrict(source_field, agg_map):
    return lax.map(restrict_layer, (source_field, agg_map))


def prolong_layer(pair):
    flat_potential = pair[0].reshape(-1)
    labels_all = pair[1]
    height = labels_all.shape[0]
    breadth = labels_all.shape[1]
    labels = jnp.arange(CGX * CGY, dtype=jnp.int32)

    def spread(block_labels):
        onehot = (block_labels[:, None] == labels[None, :]).astype(jnp.float32)
        return jnp.dot(
            onehot,
            flat_potential,
            precision=lax.Precision.HIGHEST,
            preferred_element_type=jnp.float32,
        )

    return lax.map(spread, labels_all.reshape(height // 8, 8 * breadth)).reshape(height, breadth)


def precondition(residual, diagonal, agg_map, coarse_diag, whole_diag):
    coarse_rhs = restrict(residual, agg_map)
    potential = RELAXATION * coarse_rhs / coarse_diag
    for sweep_turn in range(SWEEPS - 1):
        padded = with_halo(potential, (("tx", 1), ("ty", 2)), 1)
        potential = coarse_sweep(potential, coarse_rhs, coarse_diag, padded)
    return (residual / diagonal + lax.map(prolong_layer, (potential, agg_map)), whole_diag)


def inner_sum(residual, smoothed):
    return lax.psum(jnp.sum(residual * smoothed), ("layer", "tx", "ty"))


def body(shunt_conductance, agg_map, slot_current, slot_node, slot_count):
    height = shunt_conductance.shape[1]
    breadth = shunt_conductance.shape[2]
    tile_count = slot_count.shape[3]
    capacity = slot_current.shape[4]
    live_mask = lax.broadcasted_iota(jnp.int32, slot_current.shape, 4) < slot_count[..., None]
    currents = jnp.where(live_mask, slot_current, jnp.zeros_like(slot_current))
    targets = slot_node.astype(jnp.float32)
    arrived_current, arrived_target = (
        lax.all_to_all(
            currents.reshape(tile_count, capacity),
            ("tx", "ty"),
            split_axis=0,
            concat_axis=0,
            tiled=True,
        ),
        lax.all_to_all(
            targets.reshape(tile_count, capacity),
            ("tx", "ty"),
            split_axis=0,
            concat_axis=0,
            tiled=True,
        ),
    )
    node_ids = arrived_target.reshape(-1).astype(jnp.int32)
    sources = (
        jnp.zeros((height * breadth,), jnp.float32).at[node_ids].add(arrived_current.reshape(-1))
    )
    sources = sources.reshape(1, height, breadth)
    diagonal = shunt_conductance + (4.0 + 2.0 * VIA_CONDUCTANCE)
    coarse_diag = 4.0 * COARSE_EDGE + restrict(shunt_conductance + 2.0 * VIA_CONDUCTANCE, agg_map)
    voltage = jnp.zeros_like(sources)
    residual = sources
    smoothed, whole_diag = precondition(residual, diagonal, agg_map, coarse_diag, None)
    direction = smoothed
    curv_now = inner_sum(residual, smoothed)
    for iteration in range(ITERS):
        image = operate(direction, diagonal)
        step_size = curv_now / lax.psum(jnp.sum(direction * image), ("layer", "tx", "ty"))
        voltage = voltage + step_size * direction
        residual = residual - step_size * image
        if iteration + 1 < ITERS:
            smoothed, whole_diag = precondition(
                residual, diagonal, agg_map, coarse_diag, whole_diag
            )
            curv_next = inner_sum(residual, smoothed)
            direction = smoothed + curv_next / curv_now * direction
            curv_now = curv_next
    return (voltage, residual)


def solution(mesh):
    in_specs = (
        P("layer", "tx", "ty"),
        P("layer", "tx", "ty"),
        P("layer", "tx", "ty", None, None),
        P("layer", "tx", "ty", None, None),
        P("layer", "tx", "ty", None),
    )
    out_specs = (P("layer", "tx", "ty"), P("layer", "tx", "ty"))
    return jax.shard_map(body, mesh=mesh, in_specs=in_specs, out_specs=out_specs, check_vma=False)
```

profile of v0, /device:TPU:0, one launch (start us, length us, event | category | flops | bytes accessed | tf_op | source)
XLA Modules:
  0.0 405.4 jit_solution(14586707089420401318)
XLA Ops:
  0.6 1.3 convert_element_type.23
  1.9 6.3 %all-to-all-start = ((f32[8,1,128]{2,1,0:T(1,128)}), f32[8,1,128]{2,1,0:T(1,128)S(1)}, u32[]{:S(2)}, u32[]{:S(2)}) async-start(f32[8,1,128]{2,1,0:T(1,128)} %bitcast), calls=%async_computation | async-start | bytes 8192 | tf_op jit(solution)/shard_map/all_to_all | solution.py:132
  9.0 1.7 while.130
  12.1 1.6 all-to-all-done
  13.7 3.5 all-to-all-start.1
  17.2 5.5 %all-to-all-done.1 = f32[8,1,128]{2,1,0:T(1,128)S(1)} async-done(((f32[8,1,128]{2,1,0:T(1,128)}), f32[8,1,128]{2,1,0:T(1,128)S(1)}, u32[]{:S(2)}, u32[]{:S(2)}) %all-to-all-start.1) | async-done | bytes 4128 | tf_op jit(solution)/shard_map/all_to_all | solution.py:125
  22.7 5.9 %scatter_custom_fusion = f32[4096]{0:T(1024)S(1)} fusion(s32[1024]{0:T(1024)S(1)} %bitcast.116, f32[1024]{0:T(1024)S(1)} %bitcast.115, f32[]{:T(128)} %constant.141.clone.1), kind=kCustom, calls=%fused_computation.150 | custom fusion | flops 1024 | bytes 16388 | tf_op jit(solution)/shard_map/scatter-add | solution.py:142
  28.6 1.7 while.129
  30.4 1.3 collective-permute-start
  31.7 3.0 collective-permute-start.1
  35.6 1.3 collective-permute-start.2
  36.9 4.5 %collective-permute-start.3 = (f32[1,10,1]{2,1,0:T(8,128)S(1)}, f32[1,10,1]{2,1,0:T(8,128)S(1)}, u32[]{:S(2)}, u32[]{:S(2)}) collective-permute-start(f32[1,10,1]{2,1,0:T(8,128)S(1)} %get-tuple-element.468), channel_id=1, source_target_pairs={{0,1},{1,2},{2,3},{4,5},{5,6},{6,7},{8,9},{9,10},{10,11},{12,13},{... | collective-permute-start | bytes 128 | tf_op jit(solution)/shard_map/ppermute | solution.py:22
  41.5 1.3 collective-permute-done.3
  42.9 1.3 collective-permute-start.4
  44.2 3.0 collective-permute-start.5
  49.4 4.8 %collective-permute-start.7 = (f32[1,10,1]{2,1,0:T(8,128)S(1)}, f32[1,10,1]{2,1,0:T(8,128)S(1)}, u32[]{:S(2)}, u32[]{:S(2)}) collective-permute-start(f32[1,10,1]{2,1,0:T(8,128)S(1)} %get-tuple-element.466), channel_id=1, source_target_pairs={{0,1},{1,2},{2,3},{4,5},{5,6},{6,7},{8,9},{9,10},{10,11},{12,13},{... | collective-permute-start | bytes 128 | tf_op jit(solution)/shard_map/ppermute | solution.py:22
  54.3 1.3 collective-permute-done.7
  55.8 2.2 while.126
  58.0 3.4 collective-permute-start.8
  61.4 1.3 collective-permute-start.9
  62.9 4.2 %collective-permute-done.9 = f32[1,32,128]{2,1,0:T(8,128)S(1)} collective-permute-done((f32[1,32,128]{2,1,0:T(8,128)S(1)}, f32[1,32,128]{2,1,0:T(8,128)S(1)}, u32[]{:S(2)}, u32[]{:S(2)}) %collective-permute-start.9) | collective-permute-done | bytes 16416 | tf_op jit(solution)/shard_map/ppermute | solution.py:25
  68.4 3.0 collective-permute-start.11
  72.3 1.3 collective-permute-start.12
  73.6 4.8 %collective-permute-start.13 = (f32[3,34,1]{2,1,0:T(8,128)S(1)}, f32[3,34,1]{2,1,0:T(8,128)S(1)}, u32[]{:S(2)}, u32[]{:S(2)}) collective-permute-start(f32[3,34,1]{2,1,0:T(8,128)S(1)} %get-tuple-element.450), channel_id=1, source_target_pairs={{0,1},{1,2},{2,3},{4,5},{5,6},{6,7},{8,9},{9,10},{10,11},{12,13},{... | collective-permute-start | bytes 1232 | tf_op jit(solution)/shard_map/ppermute | solution.py:22
  79.0 1.3 collective-permute-done.13
  81.0 41.4 %all-reduce = (f32[]{:T(128)}, f32[]{:T(128)}) all-reduce(f32[]{:T(128)} %get-tuple-element.381, f32[]{:T(128)} %get-tuple-element.380), channel_id=1, replica_groups=mesh['layer'=4,'tx'=2,'ty'=4] {'layer','tx','ty'}, use_global_device_ids=true, to_apply=%region_8.9 | all-reduce | flops 2 | bytes 16 | tf_op jit(solution)/shard_map/psum | solution.py:113
  123.7 1.7 while.131
  125.5 1.3 collective-permute-start.14
  126.8 3.0 collective-permute-start.15
  132.0 4.6 %collective-permute-start.17 = (f32[1,10,1]{2,1,0:T(8,128)S(1)}, f32[1,10,1]{2,1,0:T(8,128)S(1)}, u32[]{:S(2)}, u32[]{:S(2)}) collective-permute-start(f32[1,10,1]{2,1,0:T(8,128)S(1)} %get-tuple-element.464), channel_id=1, source_target_pairs={{0,1},{1,2},{2,3},{4,5},{5,6},{6,7},{8,9},{9,10},{10,11},{12,13},{... | collective-permute-start | bytes 128 | tf_op jit(solution)/shard_map/ppermute | solution.py:22
  136.6 1.3 collective-permute-done.17
  138.1 1.3 collective-permute-start.18
  139.4 3.0 collective-permute-start.19
  144.6 4.8 %collective-permute-start.21 = (f32[1,10,1]{2,1,0:T(8,128)S(1)}, f32[1,10,1]{2,1,0:T(8,128)S(1)}, u32[]{:S(2)}, u32[]{:S(2)}) collective-permute-start(f32[1,10,1]{2,1,0:T(8,128)S(1)} %get-tuple-element.462), channel_id=1, source_target_pairs={{0,1},{1,2},{2,3},{4,5},{5,6},{6,7},{8,9},{9,10},{10,11},{12,13},{... | collective-permute-start | bytes 128 | tf_op jit(solution)/shard_map/ppermute | solution.py:22
  149.4 1.3 collective-permute-done.21
  150.9 2.2 while.127
  153.7 43.3 %psum.44 = f32[]{:T(128)} all-reduce(f32[]{:T(128)} %multiply_reduce_fusion.3), channel_id=1, replica_groups=mesh['layer'=4,'tx'=2,'ty'=4] {'layer','tx','ty'}, use_global_device_ids=true, to_apply=%region_16.17 | all-reduce | flops 1 | bytes 8 | tf_op jit(solution)/shard_map/psum | solution.py:113
  198.3 4.2 %collective-permute-start.22 = (f32[1,32,128]{2,1,0:T(8,128)S(1)}, f32[1,32,128]{2,1,0:T(8,128)S(1)}, u32[]{:S(2)}, u32[]{:S(2)}) collective-permute-start(f32[1,32,128]{2,1,0:T(8,128)S(1)} %multiply_add_fusion.2), channel_id=1, source_target_pairs={{0,8},{8,16},{16,24},{1,9},{9,17},{17,25},{2,10},{10,18},{18,26},{... | collective-permute-start | bytes 49160 | tf_op jit(solution)/shard_map/ppermute | solution.py:22
  202.5 1.3 collective-permute-start.23
  204.0 4.2 %collective-permute-done.23 = f32[1,32,128]{2,1,0:T(8,128)S(1)} collective-permute-done((f32[1,32,128]{2,1,0:T(8,128)S(1)}, f32[1,32,128]{2,1,0:T(8,128)S(1)}, u32[]{:S(2)}, u32[]{:S(2)}) %collective-permute-start.23) | collective-permute-done | bytes 16416 | tf_op jit(solution)/shard_map/ppermute | solution.py:25
  209.5 3.0 collective-permute-start.25
  213.4 1.3 collective-permute-start.26
  214.7 4.5 %collective-permute-start.27 = (f32[3,34,1]{2,1,0:T(8,128)S(1)}, f32[3,34,1]{2,1,0:T(8,128)S(1)}, u32[]{:S(2)}, u32[]{:S(2)}) collective-permute-start(f32[3,34,1]{2,1,0:T(8,128)S(1)} %get-tuple-element.448), channel_id=1, source_target_pairs={{0,1},{1,2},{2,3},{4,5},{5,6},{6,7},{8,9},{9,10},{10,11},{12,13},{... | collective-permute-start | bytes 1232 | tf_op jit(solution)/shard_map/ppermute | solution.py:22
  219.8 1.3 collective-permute-done.27
  221.8 41.5 %psum.45 = f32[]{:T(128)} all-reduce(f32[]{:T(128)} %get-tuple-element.442), channel_id=1, replica_groups=mesh['layer'=4,'tx'=2,'ty'=4] {'layer','tx','ty'}, use_global_device_ids=true, to_apply=%region_18.19 | all-reduce | flops 1 | bytes 8 | tf_op jit(solution)/shard_map/psum | solution.py:154
  264.6 1.7 while.132
  266.4 1.3 collective-permute-start.28
  267.7 3.0 collective-permute-start.29
  272.9 4.5 %collective-permute-start.31 = (f32[1,10,1]{2,1,0:T(8,128)S(1)}, f32[1,10,1]{2,1,0:T(8,128)S(1)}, u32[]{:S(2)}, u32[]{:S(2)}) collective-permute-start(f32[1,10,1]{2,1,0:T(8,128)S(1)} %get-tuple-element.460), channel_id=1, source_target_pairs={{0,1},{1,2},{2,3},{4,5},{5,6},{6,7},{8,9},{9,10},{10,11},{12,13},{... | collective-permute-start | bytes 128 | tf_op jit(solution)/shard_map/ppermute | solution.py:22
  277.5 1.3 collective-permute-done.31
  278.9 1.3 collective-permute-start.32
  280.2 3.0 collective-permute-start.33
  285.4 4.8 %collective-permute-start.35 = (f32[1,10,1]{2,1,0:T(8,128)S(1)}, f32[1,10,1]{2,1,0:T(8,128)S(1)}, u32[]{:S(2)}, u32[]{:S(2)}) collective-permute-start(f32[1,10,1]{2,1,0:T(8,128)S(1)} %get-tuple-element.458), channel_id=1, source_target_pairs={{0,1},{1,2},{2,3},{4,5},{5,6},{6,7},{8,9},{9,10},{10,11},{12,13},{... | collective-permute-start | bytes 128 | tf_op jit(solution)/shard_map/ppermute | solution.py:22
  290.3 1.3 collective-permute-done.35
  291.8 2.2 while.128
  294.6 43.2 %psum.46 = f32[]{:T(128)} all-reduce(f32[]{:T(128)} %multiply_reduce_fusion.1), channel_id=1, replica_groups=mesh['layer'=4,'tx'=2,'ty'=4] {'layer','tx','ty'}, use_global_device_ids=true, to_apply=%region_24.25 | all-reduce | flops 1 | bytes 8 | tf_op jit(solution)/shard_map/psum | solution.py:113
  339.2 4.2 %collective-permute-start.36 = (f32[1,32,128]{2,1,0:T(8,128)S(1)}, f32[1,32,128]{2,1,0:T(8,128)S(1)}, u32[]{:S(2)}, u32[]{:S(2)}) collective-permute-start(f32[1,32,128]{2,1,0:T(8,128)S(1)} %multiply_add_fusion.1), channel_id=1, source_target_pairs={{0,8},{8,16},{16,24},{1,9},{9,17},{17,25},{2,10},{10,18},{18,26},{... | collective-permute-start | bytes 49160 | tf_op jit(solution)/shard_map/ppermute | solution.py:22
  343.4 1.3 collective-permute-start.37
  344.8 4.2 %collective-permute-done.37 = f32[1,32,128]{2,1,0:T(8,128)S(1)} collective-permute-done((f32[1,32,128]{2,1,0:T(8,128)S(1)}, f32[1,32,128]{2,1,0:T(8,128)S(1)}, u32[]{:S(2)}, u32[]{:S(2)}) %collective-permute-start.37) | collective-permute-done | bytes 16416 | tf_op jit(solution)/shard_map/ppermute | solution.py:25
  350.3 3.0 collective-permute-start.39
  354.2 1.3 collective-permute-start.40
  355.5 4.5 %collective-permute-start.41 = (f32[3,34,1]{2,1,0:T(8,128)S(1)}, f32[3,34,1]{2,1,0:T(8,128)S(1)}, u32[]{:S(2)}, u32[]{:S(2)}) collective-permute-start(f32[3,34,1]{2,1,0:T(8,128)S(1)} %get-tuple-element.446), channel_id=1, source_target_pairs={{0,1},{1,2},{2,3},{4,5},{5,6},{6,7},{8,9},{9,10},{10,11},{12,13},{... | collective-permute-start | bytes 1232 | tf_op jit(solution)/shard_map/ppermute | solution.py:22
  360.4 1.6 collective-permute-done.41
  362.6 40.8 %psum.47 = f32[]{:T(128)} all-reduce(f32[]{:T(128)} %get-tuple-element.440), channel_id=1, replica_groups=mesh['layer'=4,'tx'=2,'ty'=4] {'layer','tx','ty'}, use_global_device_ids=true, to_apply=%region_26.27 | all-reduce | flops 1 | bytes 8 | tf_op jit(solution)/shard_map/psum | solution.py:154
  (187 shorter events, 39.7 us)
Async XLA Ops:
  0.6 7.6 %copy-start.1 = (s32[1,32,128]{2,1,0:T(8,128)S(1)}, s32[1,32,128]{2,1,0:T(8,128)}, u32[]{:S(2)}) copy-start(s32[1,32,128]{2,1,0:T(8,128)} %param.20) | copy-start | bytes 49156
  1.9 11.8 %all-to-all-start = ((f32[8,1,128]{2,1,0:T(1,128)}), f32[8,1,128]{2,1,0:T(1,128)S(1)}, u32[]{:S(2)}, u32[]{:S(2)}) async-start(f32[8,1,128]{2,1,0:T(1,128)} %bitcast), calls=%async_computation | async-start | bytes 8192 | tf_op jit(solution)/shard_map/all_to_all | solution.py:132
  8.3 0.7 copy-start
  9.0 1.7 copy-start.2
  10.7 0.7 copy-start.3
  13.7 9.0 %all-to-all-start.1 = ((f32[8,1,128]{2,1,0:T(1,128)}), f32[8,1,128]{2,1,0:T(1,128)S(1)}, u32[]{:S(2)}, u32[]{:S(2)}) async-start(f32[8,1,128]{2,1,0:T(1,128)} %bitcast.4), calls=%async_computation.1 | async-start | bytes 8192 | tf_op jit(solution)/shard_map/all_to_all | solution.py:125
  30.4 4.3 %collective-permute-start = (f32[1,1,16]{2,1,0:T(1,128)S(1)}, f32[1,1,16]{2,1,0:T(1,128)S(1)}, u32[]{:S(2)}, u32[]{:S(2)}) collective-permute-start(f32[1,1,16]{2,1,0:T(1,128)S(1)} %get-tuple-element.480), channel_id=1, source_target_pairs={{4,0},{5,1},{6,2},{7,3},{12,8},{13,9},{14,10},{15,11},{20,16},{21,... | collective-permute-start | bytes 200 | tf_op jit(solution)/shard_map/ppermute | solution.py:25
  31.7 3.8 collective-permute-start.1
  35.6 5.8 %collective-permute-start.2 = (f32[1,10,1]{2,1,0:T(8,128)S(1)}, f32[1,10,1]{2,1,0:T(8,128)S(1)}, u32[]{:S(2)}, u32[]{:S(2)}) collective-permute-start(f32[1,10,1]{2,1,0:T(8,128)S(1)} %get-tuple-element.467), channel_id=1, source_target_pairs={{1,0},{2,1},{3,2},{5,4},{6,5},{7,6},{9,8},{10,9},{11,10},{13,12},{... | collective-permute-start | bytes 128 | tf_op jit(solution)/shard_map/ppermute | solution.py:25
  36.9 5.9 %collective-permute-start.3 = (f32[1,10,1]{2,1,0:T(8,128)S(1)}, f32[1,10,1]{2,1,0:T(8,128)S(1)}, u32[]{:S(2)}, u32[]{:S(2)}) collective-permute-start(f32[1,10,1]{2,1,0:T(8,128)S(1)} %get-tuple-element.468), channel_id=1, source_target_pairs={{0,1},{1,2},{2,3},{4,5},{5,6},{6,7},{8,9},{9,10},{10,11},{12,13},{... | collective-permute-start | bytes 128 | tf_op jit(solution)/shard_map/ppermute | solution.py:22
  42.9 4.3 %collective-permute-start.4 = (f32[1,1,16]{2,1,0:T(1,128)S(1)}, f32[1,1,16]{2,1,0:T(1,128)S(1)}, u32[]{:S(2)}, u32[]{:S(2)}) collective-permute-start(f32[1,1,16]{2,1,0:T(1,128)S(1)} %get-tuple-element.478), channel_id=1, source_target_pairs={{4,0},{5,1},{6,2},{7,3},{12,8},{13,9},{14,10},{15,11},{20,16},{21,... | collective-permute-start | bytes 200 | tf_op jit(solution)/shard_map/ppermute | solution.py:25
  44.2 3.8 collective-permute-start.5
  48.2 6.1 %collective-permute-start.6 = (f32[1,10,1]{2,1,0:T(8,128)S(1)}, f32[1,10,1]{2,1,0:T(8,128)S(1)}, u32[]{:S(2)}, u32[]{:S(2)}) collective-permute-start(f32[1,10,1]{2,1,0:T(8,128)S(1)} %get-tuple-element.465), channel_id=1, source_target_pairs={{1,0},{2,1},{3,2},{5,4},{6,5},{7,6},{9,8},{10,9},{11,10},{13,12},{... | collective-permute-start | bytes 128 | tf_op jit(solution)/shard_map/ppermute | solution.py:25
  49.4 6.2 %collective-permute-start.7 = (f32[1,10,1]{2,1,0:T(8,128)S(1)}, f32[1,10,1]{2,1,0:T(8,128)S(1)}, u32[]{:S(2)}, u32[]{:S(2)}) collective-permute-start(f32[1,10,1]{2,1,0:T(8,128)S(1)} %get-tuple-element.466), channel_id=1, source_target_pairs={{0,1},{1,2},{2,3},{4,5},{5,6},{6,7},{8,9},{9,10},{10,11},{12,13},{... | collective-permute-start | bytes 128 | tf_op jit(solution)/shard_map/ppermute | solution.py:22
  58.0 4.8 %collective-permute-start.8 = (f32[1,32,128]{2,1,0:T(8,128)S(1)}, f32[1,32,128]{2,1,0:T(8,128)S(1)}, u32[]{:S(2)}, u32[]{:S(2)}) collective-permute-start(f32[1,32,128]{2,1,0:T(8,128)S(1)} %fusion.58), channel_id=1, source_target_pairs={{0,8},{8,16},{16,24},{1,9},{9,17},{17,25},{2,10},{10,18},{18,26},{... | collective-permute-start | bytes 49160 | tf_op jit(solution)/shard_map/ppermute | solution.py:22
  61.4 5.6 %collective-permute-start.9 = (f32[1,32,128]{2,1,0:T(8,128)S(1)}, f32[1,32,128]{2,1,0:T(8,128)S(1)}, u32[]{:S(2)}, u32[]{:S(2)}) collective-permute-start(f32[1,32,128]{2,1,0:T(8,128)S(1)} %fusion.58), channel_id=1, source_target_pairs={{8,0},{16,8},{24,16},{9,1},{17,9},{25,17},{10,2},{18,10},{26,18},{... | collective-permute-start | bytes 49160 | tf_op jit(solution)/shard_map/ppermute | solution.py:25
  67.1 4.3 %collective-permute-start.10 = (f32[3,1,128]{2,1,0:T(1,128)S(1)}, f32[3,1,128]{2,1,0:T(1,128)S(1)}, u32[]{:S(2)}, u32[]{:S(2)}) collective-permute-start(f32[3,1,128]{2,1,0:T(1,128)S(1)} %get-tuple-element.456), channel_id=1, source_target_pairs={{4,0},{5,1},{6,2},{7,3},{12,8},{13,9},{14,10},{15,11},{20,16},{21,... | collective-permute-start | bytes 4616 | tf_op jit(solution)/shard_map/ppermute | solution.py:25
  68.4 3.8 collective-permute-start.11
  72.3 6.7 %collective-permute-start.12 = (f32[3,34,1]{2,1,0:T(8,128)S(1)}, f32[3,34,1]{2,1,0:T(8,128)S(1)}, u32[]{:S(2)}, u32[]{:S(2)}) collective-permute-start(f32[3,34,1]{2,1,0:T(8,128)S(1)} %get-tuple-element.449), channel_id=1, source_target_pairs={{1,0},{2,1},{3,2},{5,4},{6,5},{7,6},{9,8},{10,9},{11,10},{13,12},{... | collective-permute-start | bytes 1232 | tf_op jit(solution)/shard_map/ppermute | solution.py:25
  73.6 6.7 %collective-permute-start.13 = (f32[3,34,1]{2,1,0:T(8,128)S(1)}, f32[3,34,1]{2,1,0:T(8,128)S(1)}, u32[]{:S(2)}, u32[]{:S(2)}) collective-permute-start(f32[3,34,1]{2,1,0:T(8,128)S(1)} %get-tuple-element.450), channel_id=1, source_target_pairs={{0,1},{1,2},{2,3},{4,5},{5,6},{6,7},{8,9},{9,10},{10,11},{12,13},{... | collective-permute-start | bytes 1232 | tf_op jit(solution)/shard_map/ppermute | solution.py:22
  125.5 4.3 %collective-permute-start.14 = (f32[1,1,16]{2,1,0:T(1,128)S(1)}, f32[1,1,16]{2,1,0:T(1,128)S(1)}, u32[]{:S(2)}, u32[]{:S(2)}) collective-permute-start(f32[1,1,16]{2,1,0:T(1,128)S(1)} %get-tuple-element.476), channel_id=1, source_target_pairs={{4,0},{5,1},{6,2},{7,3},{12,8},{13,9},{14,10},{15,11},{20,16},{21,... | collective-permute-start | bytes 200 | tf_op jit(solution)/shard_map/ppermute | solution.py:25
  126.8 3.8 collective-permute-start.15
  130.7 5.9 %collective-permute-start.16 = (f32[1,10,1]{2,1,0:T(8,128)S(1)}, f32[1,10,1]{2,1,0:T(8,128)S(1)}, u32[]{:S(2)}, u32[]{:S(2)}) collective-permute-start(f32[1,10,1]{2,1,0:T(8,128)S(1)} %get-tuple-element.463), channel_id=1, source_target_pairs={{1,0},{2,1},{3,2},{5,4},{6,5},{7,6},{9,8},{10,9},{11,10},{13,12},{... | collective-permute-start | bytes 128 | tf_op jit(solution)/shard_map/ppermute | solution.py:25
  132.0 6.0 %collective-permute-start.17 = (f32[1,10,1]{2,1,0:T(8,128)S(1)}, f32[1,10,1]{2,1,0:T(8,128)S(1)}, u32[]{:S(2)}, u32[]{:S(2)}) collective-permute-start(f32[1,10,1]{2,1,0:T(8,128)S(1)} %get-tuple-element.464), channel_id=1, source_target_pairs={{0,1},{1,2},{2,3},{4,5},{5,6},{6,7},{8,9},{9,10},{10,11},{12,13},{... | collective-permute-start | bytes 128 | tf_op jit(solution)/shard_map/ppermute | solution.py:22
  138.1 4.3 %collective-permute-start.18 = (f32[1,1,16]{2,1,0:T(1,128)S(1)}, f32[1,1,16]{2,1,0:T(1,128)S(1)}, u32[]{:S(2)}, u32[]{:S(2)}) collective-permute-start(f32[1,1,16]{2,1,0:T(1,128)S(1)} %get-tuple-element.474), channel_id=1, source_target_pairs={{4,0},{5,1},{6,2},{7,3},{12,8},{13,9},{14,10},{15,11},{20,16},{21,... | collective-permute-start | bytes 200 | tf_op jit(solution)/shard_map/ppermute | solution.py:25
  139.4 3.8 collective-permute-start.19
  143.3 6.1 %collective-permute-start.20 = (f32[1,10,1]{2,1,0:T(8,128)S(1)}, f32[1,10,1]{2,1,0:T(8,128)S(1)}, u32[]{:S(2)}, u32[]{:S(2)}) collective-permute-start(f32[1,10,1]{2,1,0:T(8,128)S(1)} %get-tuple-element.461), channel_id=1, source_target_pairs={{1,0},{2,1},{3,2},{5,4},{6,5},{7,6},{9,8},{10,9},{11,10},{13,12},{... | collective-permute-start | bytes 128 | tf_op jit(solution)/shard_map/ppermute | solution.py:25
  144.6 6.2 %collective-permute-start.21 = (f32[1,10,1]{2,1,0:T(8,128)S(1)}, f32[1,10,1]{2,1,0:T(8,128)S(1)}, u32[]{:S(2)}, u32[]{:S(2)}) collective-permute-start(f32[1,10,1]{2,1,0:T(8,128)S(1)} %get-tuple-element.462), channel_id=1, source_target_pairs={{0,1},{1,2},{2,3},{4,5},{5,6},{6,7},{8,9},{9,10},{10,11},{12,13},{... | collective-permute-start | bytes 128 | tf_op jit(solution)/shard_map/ppermute | solution.py:22
  198.3 5.6 %collective-permute-start.22 = (f32[1,32,128]{2,1,0:T(8,128)S(1)}, f32[1,32,128]{2,1,0:T(8,128)S(1)}, u32[]{:S(2)}, u32[]{:S(2)}) collective-permute-start(f32[1,32,128]{2,1,0:T(8,128)S(1)} %multiply_add_fusion.2), channel_id=1, source_target_pairs={{0,8},{8,16},{16,24},{1,9},{9,17},{17,25},{2,10},{10,18},{18,26},{... | collective-permute-start | bytes 49160 | tf_op jit(solution)/shard_map/ppermute | solution.py:22
  202.5 5.6 %collective-permute-start.23 = (f32[1,32,128]{2,1,0:T(8,128)S(1)}, f32[1,32,128]{2,1,0:T(8,128)S(1)}, u32[]{:S(2)}, u32[]{:S(2)}) collective-permute-start(f32[1,32,128]{2,1,0:T(8,128)S(1)} %multiply_add_fusion.2), channel_id=1, source_target_pairs={{8,0},{16,8},{24,16},{9,1},{17,9},{25,17},{10,2},{18,10},{26,18},{... | collective-permute-start | bytes 49160 | tf_op jit(solution)/shard_map/ppermute | solution.py:25
  208.2 4.3 %collective-permute-start.24 = (f32[3,1,128]{2,1,0:T(1,128)S(1)}, f32[3,1,128]{2,1,0:T(1,128)S(1)}, u32[]{:S(2)}, u32[]{:S(2)}) collective-permute-start(f32[3,1,128]{2,1,0:T(1,128)S(1)} %get-tuple-element.454), channel_id=1, source_target_pairs={{4,0},{5,1},{6,2},{7,3},{12,8},{13,9},{14,10},{15,11},{20,16},{21,... | collective-permute-start | bytes 4616 | tf_op jit(solution)/shard_map/ppermute | solution.py:25
  209.5 3.8 collective-permute-start.25
  213.4 6.4 %collective-permute-start.26 = (f32[3,34,1]{2,1,0:T(8,128)S(1)}, f32[3,34,1]{2,1,0:T(8,128)S(1)}, u32[]{:S(2)}, u32[]{:S(2)}) collective-permute-start(f32[3,34,1]{2,1,0:T(8,128)S(1)} %get-tuple-element.447), channel_id=1, source_target_pairs={{1,0},{2,1},{3,2},{5,4},{6,5},{7,6},{9,8},{10,9},{11,10},{13,12},{... | collective-permute-start | bytes 1232 | tf_op jit(solution)/shard_map/ppermute | solution.py:25
  214.7 6.4 %collective-permute-start.27 = (f32[3,34,1]{2,1,0:T(8,128)S(1)}, f32[3,34,1]{2,1,0:T(8,128)S(1)}, u32[]{:S(2)}, u32[]{:S(2)}) collective-permute-start(f32[3,34,1]{2,1,0:T(8,128)S(1)} %get-tuple-element.448), channel_id=1, source_target_pairs={{0,1},{1,2},{2,3},{4,5},{5,6},{6,7},{8,9},{9,10},{10,11},{12,13},{... | collective-permute-start | bytes 1232 | tf_op jit(solution)/shard_map/ppermute | solution.py:22
  266.4 4.3 %collective-permute-start.28 = (f32[1,1,16]{2,1,0:T(1,128)S(1)}, f32[1,1,16]{2,1,0:T(1,128)S(1)}, u32[]{:S(2)}, u32[]{:S(2)}) collective-permute-start(f32[1,1,16]{2,1,0:T(1,128)S(1)} %get-tuple-element.472), channel_id=1, source_target_pairs={{4,0},{5,1},{6,2},{7,3},{12,8},{13,9},{14,10},{15,11},{20,16},{21,... | collective-permute-start | bytes 200 | tf_op jit(solution)/shard_map/ppermute | solution.py:25
  267.7 3.8 collective-permute-start.29
  271.6 5.8 %collective-permute-start.30 = (f32[1,10,1]{2,1,0:T(8,128)S(1)}, f32[1,10,1]{2,1,0:T(8,128)S(1)}, u32[]{:S(2)}, u32[]{:S(2)}) collective-permute-start(f32[1,10,1]{2,1,0:T(8,128)S(1)} %get-tuple-element.459), channel_id=1, source_target_pairs={{1,0},{2,1},{3,2},{5,4},{6,5},{7,6},{9,8},{10,9},{11,10},{13,12},{... | collective-permute-start | bytes 128 | tf_op jit(solution)/shard_map/ppermute | solution.py:25
  272.9 5.9 %collective-permute-start.31 = (f32[1,10,1]{2,1,0:T(8,128)S(1)}, f32[1,10,1]{2,1,0:T(8,128)S(1)}, u32[]{:S(2)}, u32[]{:S(2)}) collective-permute-start(f32[1,10,1]{2,1,0:T(8,128)S(1)} %get-tuple-element.460), channel_id=1, source_target_pairs={{0,1},{1,2},{2,3},{4,5},{5,6},{6,7},{8,9},{9,10},{10,11},{12,13},{... | collective-permute-start | bytes 128 | tf_op jit(solution)/shard_map/ppermute | solution.py:22
  278.9 4.3 %collective-permute-start.32 = (f32[1,1,16]{2,1,0:T(1,128)S(1)}, f32[1,1,16]{2,1,0:T(1,128)S(1)}, u32[]{:S(2)}, u32[]{:S(2)}) collective-permute-start(f32[1,1,16]{2,1,0:T(1,128)S(1)} %get-tuple-element.470), channel_id=1, source_target_pairs={{4,0},{5,1},{6,2},{7,3},{12,8},{13,9},{14,10},{15,11},{20,16},{21,... | collective-permute-start | bytes 200 | tf_op jit(solution)/shard_map/ppermute | solution.py:25
  280.2 3.8 collective-permute-start.33
  284.1 6.1 %collective-permute-start.34 = (f32[1,10,1]{2,1,0:T(8,128)S(1)}, f32[1,10,1]{2,1,0:T(8,128)S(1)}, u32[]{:S(2)}, u32[]{:S(2)}) collective-permute-start(f32[1,10,1]{2,1,0:T(8,128)S(1)} %get-tuple-element.457), channel_id=1, source_target_pairs={{1,0},{2,1},{3,2},{5,4},{6,5},{7,6},{9,8},{10,9},{11,10},{13,12},{... | collective-permute-start | bytes 128 | tf_op jit(solution)/shard_map/ppermute | solution.py:25
  285.4 6.2 %collective-permute-start.35 = (f32[1,10,1]{2,1,0:T(8,128)S(1)}, f32[1,10,1]{2,1,0:T(8,128)S(1)}, u32[]{:S(2)}, u32[]{:S(2)}) collective-permute-start(f32[1,10,1]{2,1,0:T(8,128)S(1)} %get-tuple-element.458), channel_id=1, source_target_pairs={{0,1},{1,2},{2,3},{4,5},{5,6},{6,7},{8,9},{9,10},{10,11},{12,13},{... | collective-permute-start | bytes 128 | tf_op jit(solution)/shard_map/ppermute | solution.py:22
  339.2 5.6 %collective-permute-start.36 = (f32[1,32,128]{2,1,0:T(8,128)S(1)}, f32[1,32,128]{2,1,0:T(8,128)S(1)}, u32[]{:S(2)}, u32[]{:S(2)}) collective-permute-start(f32[1,32,128]{2,1,0:T(8,128)S(1)} %multiply_add_fusion.1), channel_id=1, source_target_pairs={{0,8},{8,16},{16,24},{1,9},{9,17},{17,25},{2,10},{10,18},{18,26},{... | collective-permute-start | bytes 49160 | tf_op jit(solution)/shard_map/ppermute | solution.py:22
  343.4 5.6 %collective-permute-start.37 = (f32[1,32,128]{2,1,0:T(8,128)S(1)}, f32[1,32,128]{2,1,0:T(8,128)S(1)}, u32[]{:S(2)}, u32[]{:S(2)}) collective-permute-start(f32[1,32,128]{2,1,0:T(8,128)S(1)} %multiply_add_fusion.1), channel_id=1, source_target_pairs={{8,0},{16,8},{24,16},{9,1},{17,9},{25,17},{10,2},{18,10},{26,18},{... | collective-permute-start | bytes 49160 | tf_op jit(solution)/shard_map/ppermute | solution.py:25
  349.0 4.3 %collective-permute-start.38 = (f32[3,1,128]{2,1,0:T(1,128)S(1)}, f32[3,1,128]{2,1,0:T(1,128)S(1)}, u32[]{:S(2)}, u32[]{:S(2)}) collective-permute-start(f32[3,1,128]{2,1,0:T(1,128)S(1)} %get-tuple-element.452), channel_id=1, source_target_pairs={{4,0},{5,1},{6,2},{7,3},{12,8},{13,9},{14,10},{15,11},{20,16},{21,... | collective-permute-start | bytes 4616 | tf_op jit(solution)/shard_map/ppermute | solution.py:25
  350.3 3.8 collective-permute-start.39
  354.2 6.1 %collective-permute-start.40 = (f32[3,34,1]{2,1,0:T(8,128)S(1)}, f32[3,34,1]{2,1,0:T(8,128)S(1)}, u32[]{:S(2)}, u32[]{:S(2)}) collective-permute-start(f32[3,34,1]{2,1,0:T(8,128)S(1)} %get-tuple-element.445), channel_id=1, source_target_pairs={{1,0},{2,1},{3,2},{5,4},{6,5},{7,6},{9,8},{10,9},{11,10},{13,12},{... | collective-permute-start | bytes 1232 | tf_op jit(solution)/shard_map/ppermute | solution.py:25
  355.5 6.4 %collective-permute-start.41 = (f32[3,34,1]{2,1,0:T(8,128)S(1)}, f32[3,34,1]{2,1,0:T(8,128)S(1)}, u32[]{:S(2)}, u32[]{:S(2)}) collective-permute-start(f32[3,34,1]{2,1,0:T(8,128)S(1)} %get-tuple-element.446), channel_id=1, source_target_pairs={{0,1},{1,2},{2,3},{4,5},{5,6},{6,7},{8,9},{9,10},{10,11},{12,13},{... | collective-permute-start | bytes 1232 | tf_op jit(solution)/shard_map/ppermute | solution.py:22
where the time goes:
time: 407 us; the launch traced here: 405 us
  blocking collectives  210 us (52%)
  starting transfers between devices  118 us (29%)
  waiting for transfers between devices  40.8 us (10%)
  other arithmetic  12.5 us (3%)
  matrix products  11.4 us (3%)
  between operations  7.97 us (2%)
    psum x3, blocking collectives, inner_sum(): return lax.psum(jnp.sum(residual * smoothed), ('layer', 'tx', 'ty'))  128 us
    psum x2, blocking collectives, body(): lax.psum(jnp.sum(direction * image), ('layer', 'tx', 'ty'))  82.3 us
    ppermute x21, starting transfers between devices, with_halo(): lax.ppermute(lax.slice_in_dim(block, block.shape[dim] - width, None, axis...  81.1 us
    ppermute x21, starting transfers between devices, with_halo(): lax.ppermute(lax.slice_in_dim(block, 0, width, axis=dim), axis, backward)  27 us
    ppermute x21, waiting for transfers between devices, with_halo(): lax.ppermute(lax.slice_in_dim(block, block.shape[dim] - width, None, axis...  19.7 us
    ppermute x21, waiting for transfers between devices, with_halo(): lax.ppermute(lax.slice_in_dim(block, 0, width, axis=dim), axis, backward)  14 us
  transfers between devices with their start and end apart: 44, of which 29 were waited for; matrix products, arithmetic and copies ran while one was open for 1% of the time, Pallas kernels for 0%

commit v1 on v0

v1 whole, which is shorter than its diff:
```python
import functools

import jax
import jax.numpy as jnp
from jax import lax
from jax.experimental import pallas as pl
from jax.experimental.pallas import tpu as pltpu
from jax.sharding import PartitionSpec as P

CGX = 8
CGY = 16
ITERS = 3
SWEEPS = 3
VIA_CONDUCTANCE = 0.5
COARSE_EDGE = 8.0
RELAXATION = 0.6
SHIFT = 1.25
MESH = pl.DeviceIdType.MESH
AROUND = [(a, b) for a in (-1, 0, 1) for b in (-1, 0, 1)]
SIDES = [(-1, 0, 0), (1, 0, 0), (0, -1, 0), (0, 1, 0), (0, 0, -1), (0, 0, 1)]


def iota(shape, dim):
    return lax.broadcasted_iota(jnp.int32, shape, dim)


def each(count, step):
    if count <= 8:
        for k in range(1, count):
            step(k)
    else:
        def run(k, carry):
            step(k)
            return carry

        lax.fori_loop(1, count, run, 0)


def quadratic(moments, coefs):
    total = 0.0
    for i, a in enumerate(coefs):
        for j, b in enumerate(coefs):
            total = total + a * b * moments[i + j]
    return total


def kernel(
    dims,
    shunt_ref, agg_ref, current_ref, node_ref, count_ref,
    voltage_ref, residual_ref,
    msg, box, row_hot, col_hot, coarse_out, coarse_in, field_out, field_in,
    part_out, part_tile, part_layer,
    msg_s, msg_r, coarse_s, coarse_r, field_s, field_r, tile_s, tile_r, layer_s, layer_r,
):
    layers, n_tx, n_ty = dims
    tiles = n_tx * n_ty
    height, breadth = shunt_ref.shape[1], shunt_ref.shape[2]
    lay = lax.axis_index("layer")
    tx = lax.axis_index("tx")
    ty = lax.axis_index("ty")
    me = tx * n_ty + ty

    def tile_device(d):
        return {"layer": lay, "tx": d // n_ty, "ty": lax.rem(d, n_ty)}

    def layer_device(l):
        return {"layer": l, "tx": tx, "ty": ty}

    def beside_layer(da, dx, dy):
        here = True
        for value, delta, size in ((lay, da, layers), (tx, dx, n_tx), (ty, dy, n_ty)):
            if delta < 0:
                here = jnp.logical_and(here, value > 0)
            if delta > 0:
                here = jnp.logical_and(here, value < size - 1)
        return here

    barrier = pltpu.get_barrier_semaphore()
    each(tiles, lambda k: pl.semaphore_signal(
        barrier, inc=1, device_id=tile_device(lax.rem(me + k, tiles)), device_id_type=MESH))
    each(layers, lambda k: pl.semaphore_signal(
        barrier, inc=1, device_id=layer_device(lax.rem(lay + k, layers)), device_id_type=MESH))

    for k, (a, b) in enumerate(AROUND):
        if (a, b) != (0, 0):
            @pl.when(jnp.logical_not(beside_layer(0, a, b)))
            def _(k=k):
                coarse_in[:, k] = jnp.zeros((ITERS + 1,) + coarse_in.shape[2:], jnp.float32)
    for k, side in enumerate(SIDES):
        @pl.when(jnp.logical_not(beside_layer(*side)))
        def _(k=k):
            field_in[:, k] = jnp.zeros((ITERS,) + field_in.shape[2:], jnp.float32)

    square = (tiles, tiles)
    counts = jnp.broadcast_to(count_ref[0, 0].astype(jnp.float32), square)
    counts = jnp.sum(
        jnp.where(iota(square, 0) == iota(square, 1), counts, 0.0), axis=1, keepdims=True)
    slots = current_ref.shape[3:]
    msg[:, 0, :] = jnp.where(iota(slots, 1).astype(jnp.float32) < counts, current_ref[0, 0, 0], 0.0)
    msg[:, 1, :] = node_ref[0, 0, 0].astype(jnp.float32)

    pl.semaphore_wait(barrier, tiles + layers - 2)

    def slot_copy(k):
        return pltpu.make_async_remote_copy(
            src_ref=msg.at[lax.rem(me + k, tiles)], dst_ref=box.at[me],
            send_sem=msg_s.at[k], recv_sem=msg_r.at[k],
            device_id=tile_device(lax.rem(me + k, tiles)), device_id_type=MESH)

    def slot_arrival(k):
        return pltpu.make_async_remote_copy(
            src_ref=msg.at[me], dst_ref=box.at[lax.rem(me + tiles - k, tiles)],
            send_sem=msg_s.at[k], recv_sem=msg_r.at[k],
            device_id=tile_device(lax.rem(me + k, tiles)), device_id_type=MESH)

    each(tiles, lambda k: slot_copy(k).start())
    box[me] = msg[me]

    agg = agg_ref[0]
    agg_p = agg // CGY
    agg_q = agg % CGY
    for i in range(height):
        hot = agg_p[i:i + 1, :] == iota((CGX, breadth), 0)
        row_hot[i] = jnp.where(hot, 1.0, 0.0)
        hot = agg_q[i:i + 1, :] == iota((CGY, breadth), 0)
        ch, half = i // 2, i % 2
        col_hot[CGY * ch:CGY * (ch + 1), breadth * half:breadth * (half + 1)] = jnp.where(
            hot, 1.0, 0.0).astype(jnp.bfloat16)

    lane = iota((CGX, breadth), 1)
    group = lane // CGY
    shift_sub = pltpu.roll

    def restrict(v):
        high = v.astype(jnp.bfloat16).astype(jnp.float32)
        low = v - high
        rows = []
        for ch in range(height // 2):
            cols = []
            for i in (2 * ch, 2 * ch + 1):
                mask = row_hot[i]
                cols.append(jnp.concatenate(
                    [mask * high[i:i + 1, :], mask * low[i:i + 1, :]], axis=0
                ).astype(jnp.bfloat16))
            rows.append(jnp.concatenate(cols, axis=1))
        left = jnp.concatenate(rows, axis=0)
        full = lax.dot_general(
            left, col_hot[...], (((1,), (1,)), ((), ())), preferred_element_type=jnp.float32)
        total = jnp.zeros((CGX, breadth), jnp.float32)
        for ch in range(height // 2):
            at = breadth * (ch // 8)
            piece = full[16 * ch:16 * ch + 8, at:at + breadth] + full[
                16 * ch + 8:16 * ch + 16, at:at + breadth]
            total = total + jnp.where(group == ch % 8, piece, 0.0)
        for shift in (64, 32, 16):
            total = total + pltpu.roll(total, shift, 1)
        return total

    def coarse_copy(turn, k):
        a, b = AROUND[k]
        return pltpu.make_async_remote_copy(
            src_ref=coarse_out.at[turn], dst_ref=coarse_in.at[turn, 8 - k],
            send_sem=coarse_s.at[turn, k], recv_sem=coarse_r.at[turn, 8 - k],
            device_id={"layer": lay, "tx": tx + a, "ty": ty + b}, device_id_type=MESH)

    def coarse_arrival(turn, k):
        a, b = AROUND[k]
        return pltpu.make_async_remote_copy(
            src_ref=coarse_out.at[turn], dst_ref=coarse_in.at[turn, k],
            send_sem=coarse_s.at[turn, k], recv_sem=coarse_r.at[turn, k],
            device_id={"layer": lay, "tx": tx + a, "ty": ty + b}, device_id_type=MESH)

    def coarse_each(step):
        for k, (a, b) in enumerate(AROUND):
            if (a, b) != (0, 0):
                @pl.when(beside_layer(0, a, b))
                def _(k=k):
                    step(k)

    def coarse_block(turn, own):
        rows = []
        for a in range(3):
            west = coarse_in[turn, 3 * a]
            mid = own if a == 1 else coarse_in[turn, 3 * a + 1]
            east = coarse_in[turn, 3 * a + 2]
            row = jnp.where(group == 0, west, jnp.where(group == 1, mid, east))
            rows.append(jnp.where(group < 3, row, 0.0))
        return jnp.concatenate(rows, axis=0)

    def side_part(k, ref):
        if k == 2:
            return ref.at[0:8]
        if k == 3:
            return ref.at[height - 8:height]
        return ref

    def field_copy(turn, k):
        da, dx, dy = SIDES[k]
        return pltpu.make_async_remote_copy(
            src_ref=side_part(k, field_out.at[turn]),
            dst_ref=side_part(k, field_in.at[turn, k ^ 1]),
            send_sem=field_s.at[turn, k], recv_sem=field_r.at[turn, k ^ 1],
            device_id={"layer": lay + da, "tx": tx + dx, "ty": ty + dy}, device_id_type=MESH)

    def field_arrival(turn, k):
        da, dx, dy = SIDES[k]
        return pltpu.make_async_remote_copy(
            src_ref=side_part(k ^ 1, field_out.at[turn]),
            dst_ref=side_part(k ^ 1, field_in.at[turn, k]),
            send_sem=field_s.at[turn, k], recv_sem=field_r.at[turn, k],
            device_id={"layer": lay + da, "tx": tx + dx, "ty": ty + dy}, device_id_type=MESH)

    def field_each(step):
        for k, side in enumerate(SIDES):
            @pl.when(beside_layer(*side))
            def _(k=k):
                step(k)

    shunt = shunt_ref[0]
    diagonal = shunt + (4.0 + 2.0 * VIA_CONDUCTANCE)
    own_diag = 4.0 * COARSE_EDGE + restrict(shunt + 2.0 * VIA_CONDUCTANCE)
    coarse_out[ITERS] = own_diag
    coarse_each(lambda k: coarse_copy(ITERS, k).start())
    inverse = 1.0 / diagonal

    each(tiles, lambda k: slot_arrival(k).wait_recv())

    def scatter(first):
        lefts, rights = [], []
        for k in range(8):
            amount = box[first + k, 0:1, :]
            node = box[first + k, 1:2, :].astype(jnp.int32)
            row = node // breadth
            col = node % breadth
            hot = iota((height, breadth), 0) == row
            parts = []
            for _ in range(3):
                rounded = amount.astype(jnp.bfloat16).astype(jnp.float32)
                parts.append(jnp.where(hot, rounded, 0.0).astype(jnp.bfloat16))
                amount = amount - rounded
            lefts.append(jnp.concatenate(parts, axis=0))
            hot = iota((breadth, breadth), 0) == col
            rights.append(jnp.where(hot, 1.0, 0.0).astype(jnp.bfloat16))
        full = lax.dot_general(
            jnp.concatenate(lefts, axis=1), jnp.concatenate(rights, axis=1),
            (((1,), (1,)), ((), ())), preferred_element_type=jnp.float32)
        return full[:height] + full[height:2 * height] + full[2 * height:]

    if tiles == 8:
        sources = scatter(0)
    else:
        sources = lax.fori_loop(
            0, tiles // 8, lambda g, total: total + scatter(8 * g),
            jnp.zeros((height, breadth), jnp.float32))

    big = (height, breadth)
    big_lane = iota(big, 1)
    big_row = iota(big, 0)
    power = sources
    powers, smooths = [sources], []
    for turn in range(ITERS):
        own = restrict(power)
        coarse_out[turn] = own
        coarse_each(lambda k: coarse_copy(turn, k).start())
        local = power * inverse
        if turn == 0:
            coarse_each(lambda k: coarse_arrival(ITERS, k).wait_recv())
            coarse_diag = coarse_block(ITERS, own_diag)
            coarse_inverse = jnp.where(
                coarse_diag > 0.0, RELAXATION / jnp.maximum(coarse_diag, 1.0), 0.0)
        coarse_each(lambda k: coarse_arrival(turn, k).wait_recv())
        rhs = coarse_block(turn, own)
        potential = rhs * coarse_inverse
        for sweep in range(SWEEPS - 1):
            beside = (
                pltpu.roll(potential, 1, 1) + pltpu.roll(potential, breadth - 1, 1)
                + pltpu.roll(potential, 1, 0) + pltpu.roll(potential, 3 * CGX - 1, 0))
            potential = potential + coarse_inverse * (
                rhs - (coarse_diag * potential - COARSE_EDGE * beside))
        table = jnp.where(group == 1, potential[CGX:2 * CGX], 0.0)
        for shift in (16, 32, 64):
            table = table + pltpu.roll(table, shift, 1)
        table = jnp.where(group == iota((CGX, breadth), 0), table, 0.0)
        for shift in (4, 2, 1):
            table = table + pltpu.roll(table, shift, 0)
        smooth = local + jnp.concatenate(
            [jnp.take_along_axis(table, agg[8 * i:8 * i + 8], axis=1, mode="promise_in_bounds")
             for i in range(height // 8)], axis=0)
        field_out[turn] = smooth
        field_each(lambda k: field_copy(turn, k).start())
        field_each(lambda k: field_arrival(turn, k).wait_recv())
        north = jnp.where(
            big_row == 0, field_in[turn, 2, height - 1:height, :], pltpu.roll(smooth, 1, 0))
        south = jnp.where(
            big_row == height - 1, field_in[turn, 3, 0:1, :], pltpu.roll(smooth, height - 1, 0))
        west = pltpu.roll(
            jnp.where(big_lane == breadth - 1, field_in[turn, 4], smooth), 1, 1)
        east = pltpu.roll(
            jnp.where(big_lane == 0, field_in[turn, 5], smooth), breadth - 1, 1)
        image = (diagonal * smooth - (north + south + west + east)
                 - VIA_CONDUCTANCE * (field_in[turn, 0] + field_in[turn, 1]))
        power = image - SHIFT * power
        powers.append(power)
        smooths.append(smooth)

    for k in range(2 * ITERS):
        product = powers[(k + 1) // 2] * smooths[k // 2]
        part_out[0, k:k + 1, :] = jnp.sum(product, axis=0, keepdims=True)
    part_out[0, 6:8, :] = jnp.zeros((2, breadth), jnp.float32)

    def tile_copy(k):
        return pltpu.make_async_remote_copy(
            src_ref=part_out.at[0], dst_ref=part_tile.at[me],
            send_sem=tile_s.at[k], recv_sem=tile_r.at[k],
            device_id=tile_device(lax.rem(me + k, tiles)), device_id_type=MESH)

    def tile_arrival(k):
        return pltpu.make_async_remote_copy(
            src_ref=part_out.at[0], dst_ref=part_tile.at[lax.rem(me + tiles - k, tiles)],
            send_sem=tile_s.at[k], recv_sem=tile_r.at[k],
            device_id=tile_device(lax.rem(me + k, tiles)), device_id_type=MESH)

    def layer_copy(k):
        return pltpu.make_async_remote_copy(
            src_ref=part_out.at[1], dst_ref=part_layer.at[lay],
            send_sem=layer_s.at[k], recv_sem=layer_r.at[k],
            device_id=layer_device(lax.rem(lay + k, layers)), device_id_type=MESH)

    def layer_arrival(k):
        return pltpu.make_async_remote_copy(
            src_ref=part_out.at[1], dst_ref=part_layer.at[lax.rem(lay + layers - k, layers)],
            send_sem=layer_s.at[k], recv_sem=layer_r.at[k],
            device_id=layer_device(lax.rem(lay + k, layers)), device_id_type=MESH)

    each(tiles, lambda k: tile_copy(k).start())
    part_tile[me] = part_out[0]
    each(tiles, lambda k: tile_arrival(k).wait_recv())
    part_out[1] = jnp.sum(part_tile[...], axis=0)
    each(layers, lambda k: layer_copy(k).start())
    part_layer[lay] = part_out[1]
    each(layers, lambda k: layer_arrival(k).wait_recv())
    sums = jnp.sum(jnp.sum(part_layer[...], axis=0), axis=1, keepdims=True)
    moments = [sums[k:k + 1, :] for k in range(2 * ITERS)]
    energies = [moments[k + 1] + SHIFT * moments[k] for k in range(2 * ITERS - 1)]

    res, way, volt = [1.0], [1.0], []
    curv = moments[0]
    for turn in range(ITERS):
        step = curv / quadratic(energies, way)
        volt = [(volt[i] if i < len(volt) else 0.0) + step * way[i] for i in range(turn + 1)]
        image = [0.0] * (turn + 2)
        for i in range(turn + 1):
            image[i + 1] = image[i + 1] + way[i]
            image[i] = image[i] + SHIFT * way[i]
        res = [(res[i] if i < len(res) else 0.0) - step * image[i] for i in range(turn + 2)]
        if turn + 1 < ITERS:
            newer = quadratic(moments, res)
            ratio = newer / curv
            way = [res[i] + (ratio * way[i] if i < len(way) else 0.0) for i in range(turn + 2)]
            curv = newer
    voltage = volt[0] * smooths[0]
    residual = res[0] * powers[0]
    for i in range(1, ITERS):
        voltage = voltage + volt[i] * smooths[i]
    for i in range(1, ITERS + 1):
        residual = residual + res[i] * powers[i]
    voltage_ref[0] = voltage
    residual_ref[0] = residual

    each(tiles, lambda k: slot_copy(k).wait_send())
    for turn in range(ITERS + 1):
        coarse_each(lambda k: coarse_copy(turn, k).wait_send())
    for turn in range(ITERS):
        field_each(lambda k: field_copy(turn, k).wait_send())
    each(tiles, lambda k: tile_copy(k).wait_send())
    each(layers, lambda k: layer_copy(k).wait_send())


def solution(mesh):
    layers, n_tx, n_ty = mesh.shape["layer"], mesh.shape["tx"], mesh.shape["ty"]
    tiles = n_tx * n_ty

    def body(shunt, agg, current, node, count):
        height, breadth = shunt.shape[1], shunt.shape[2]
        f32 = jnp.float32
        dma = pltpu.SemaphoreType.DMA
        vmem = pl.BlockSpec(memory_space=pltpu.VMEM)
        return tuple(pl.pallas_call(
            functools.partial(kernel, (layers, n_tx, n_ty)),
            out_shape=[jax.ShapeDtypeStruct(shunt.shape, f32)] * 2,
            in_specs=[vmem] * 5,
            out_specs=[vmem] * 2,
            scratch_shapes=[
                pltpu.VMEM((tiles, 2, current.shape[4]), f32),
                pltpu.VMEM((tiles, 2, current.shape[4]), f32),
                pltpu.VMEM((height, CGX, breadth), f32),
                pltpu.VMEM((CGY * height // 2, 2 * breadth), jnp.bfloat16),
                pltpu.VMEM((ITERS + 1, CGX, breadth), f32),
                pltpu.VMEM((ITERS + 1, 9, CGX, breadth), f32),
                pltpu.VMEM((ITERS, height, breadth), f32),
                pltpu.VMEM((ITERS, 6, height, breadth), f32),
                pltpu.VMEM((2, 8, breadth), f32),
                pltpu.VMEM((tiles, 8, breadth), f32),
                pltpu.VMEM((layers, 8, breadth), f32),
                dma((tiles,)), dma((tiles,)),
                dma((ITERS + 1, 9)), dma((ITERS + 1, 9)),
                dma((ITERS, 6)), dma((ITERS, 6)),
                dma((tiles,)), dma((tiles,)),
                dma((layers,)), dma((layers,)),
            ],
            compiler_params=pltpu.CompilerParams(
                collective_id=0, has_side_effects=True, vmem_limit_bytes=32 * 1024 * 1024),
        )(shunt, agg, current, node, count))

    in_specs = (
        P("layer", "tx", "ty"),
        P("layer", "tx", "ty"),
        P("layer", "tx", "ty", None, None),
        P("layer", "tx", "ty", None, None),
        P("layer", "tx", "ty", None),
    )
    out_specs = (P("layer", "tx", "ty"), P("layer", "tx", "ty"))

    def run(*args):
        voltage, residual = jax.shard_map(
            body, mesh=mesh, in_specs=in_specs, out_specs=out_specs, check_vma=False)(*args)
        return voltage, residual

    return run
```

time: 407 us -> 43 us (0.11)
  blocking collectives: 210 us -> 0 us
  starting transfers between devices: 118 us -> 0 us
  waiting for transfers between devices: 40.8 us -> 0 us
  Pallas kernels: 0 us -> 37.3 us
  other arithmetic: 12.5 us -> 0 us
  matrix products: 11.4 us -> 0 us
  between operations: 7.97 us -> 0.65 us
    psum x5 -> x0, blocking collectives: 210 us -> none  [the longest x3 128 us: inner_sum(): return lax.psum(jnp.sum(residual * smoothed), ('layer', 'tx', 'ty'))]
    ppermute x42 -> x0, starting transfers between devices: 108 us -> none  [the longest x21 81.1 us: with_halo(): lax.ppermute(lax.slice_in_dim(block, block.shape[dim] - width, None, axis...]
    pallas_call x0 -> x1, Pallas kernels: none -> 37.3 us  [body(): pl.pallas_call(functools.partial(kernel, (layers, n_tx, n_ty)), out_shape...]
    ppermute x42 -> x0, waiting for transfers between devices: 33.7 us -> none  [the longest x21 19.7 us: with_halo(): lax.ppermute(lax.slice_in_dim(block, block.shape[dim] - width, None, axis...]
    dot_general x28 -> x0, matrix products: 11.4 us -> none  [the longest x16 6.07 us: accumulate(): jnp.dot(block_pair[0], onehot, precision=lax.Precision.HIGHEST, preferred...]
    all_to_all x2 -> x0, starting transfers between devices: 9.79 us -> none  [the longest x1 6.33 us: body(): lax.all_to_all(targets.reshape(tile_count, capacity), ('tx', 'ty'), split...]
    all_to_all x2 -> x0, waiting for transfers between devices: 7.11 us -> none  [the longest x1 5.48 us: body(): lax.all_to_all(currents.reshape(tile_count, capacity), ('tx', 'ty'), spli...]
    scatter-add x1 -> x0, other arithmetic: 5.92 us -> none  [body(): jnp.zeros((height * breadth,), jnp.float32).at[node_ids]]
  transfers between devices with their start and end apart: 44 -> 0, of which waited for: 29 -> 0; matrix products, arithmetic and copies ran while one was open for 1% -> 0% of each run, Pallas kernels for 0% -> 0%
where the time goes in v1:
time: 43 us; the launch traced here: 42.6 us
  Pallas kernels  37.3 us (87%)
  local copies, waits for them, and re-layouts  4.67 us (11%)
  between operations  0.65 us (2%)
    pallas_call x1, Pallas kernels, body(): pl.pallas_call(functools.partial(kernel, (layers, n_tx, n_ty)), out_shape...  37.3 us
    unnamed x12, local copies, waits for them, and re-layouts  4.67 us

profile of v1, /device:TPU:0, one launch (start us, length us, event | category | flops | bytes accessed | tf_op | source)
XLA Modules:
  0.0 42.6 jit_solution(9607986973610319178)
XLA Ops:
  0.6 0.0 copy-start
  0.6 0.7 %copy-done = f32[1,32,128]{2,1,0:T(8,128)S(1)} copy-done((f32[1,32,128]{2,1,0:T(8,128)S(1)}, f32[1,32,128]{2,1,0:T(8,128)}, u32[]{:S(2)}) %copy-start) | copy-done | bytes 16408
  1.3 0.0 copy-start.1
  1.4 0.7 %copy-done.1 = s32[1,32,128]{2,1,0:T(8,128)S(1)} copy-done((s32[1,32,128]{2,1,0:T(8,128)S(1)}, s32[1,32,128]{2,1,0:T(8,128)}, u32[]{:S(2)}) %copy-start.1) | copy-done | bytes 16408
  2.1 0.0 copy-start.2
  2.1 0.7 %copy-done.2 = f32[1,1,1,8,128]{4,3,2,1,0:T(8,128)S(1)} copy-done((f32[1,1,1,8,128]{4,3,2,1,0:T(8,128)S(1)}, f32[1,1,1,8,128]{4,3,2,1,0:T(8,128)}, u32[]{:S(2)}) %copy-start.2) | copy-done | bytes 4120
  2.8 0.0 copy-start.3
  2.8 0.7 %copy-done.3 = s32[1,1,1,8,128]{4,3,2,1,0:T(8,128)S(1)} copy-done((s32[1,1,1,8,128]{4,3,2,1,0:T(8,128)S(1)}, s32[1,1,1,8,128]{4,3,2,1,0:T(8,128)}, u32[]{:S(2)}) %copy-start.3) | copy-done | bytes 4120
  3.4 0.0 copy-start.4
  3.4 0.7 %copy-done.4 = s32[1,1,1,8]{3,2,1,0:T(1,128)S(1)} copy-done((s32[1,1,1,8]{3,2,1,0:T(1,128)S(1)}, s32[1,1,1,8]{3,2,1,0:T(1,128)}, u32[]{:S(2)}) %copy-start.4) | copy-done | bytes 56
  4.1 37.3 %shard_map.68 = (f32[1,32,128]{2,1,0:T(8,128)S(1)}, f32[1,32,128]{2,1,0:T(8,128)S(1)}) custom-call(f32[1,32,128]{2,1,0:T(8,128)S(1)} %copy-done, s32[1,32,128]{2,1,0:T(8,128)S(1)} %copy-done.1, f32[1,1,1,8,128]{4,3,2,1,0:T(8,128)S(1)} %copy-done.2, s32[1,1,1,8,128]{4,3,2,1,0:T(8,128)S(1)} %copy-done.3, s32[1,1,1,8]{3,2,1,0:T(1,128)S(1)} %copy-done.4), custom_call_target="tpu_custom_call" | custom-call | tf_op jit(solution)/shard_map/pallas_call | solution.py:388
  41.4 0.6 %copy.9 = f32[1,32,128]{2,1,0:T(8,128)} copy(f32[1,32,128]{2,1,0:T(8,128)S(1)} %get-tuple-element.4) | data formatting | bytes 32768
  42.0 0.6 %copy.10 = f32[1,32,128]{2,1,0:T(8,128)} copy(f32[1,32,128]{2,1,0:T(8,128)S(1)} %get-tuple-element.5) | data formatting | bytes 32768
Async XLA Ops:
  0.6 0.7 %copy-start = (f32[1,32,128]{2,1,0:T(8,128)S(1)}, f32[1,32,128]{2,1,0:T(8,128)}, u32[]{:S(2)}) copy-start(f32[1,32,128]{2,1,0:T(8,128)} %shunt_ref.1) | copy-start | bytes 49156
  1.3 0.7 %copy-start.1 = (s32[1,32,128]{2,1,0:T(8,128)S(1)}, s32[1,32,128]{2,1,0:T(8,128)}, u32[]{:S(2)}) copy-start(s32[1,32,128]{2,1,0:T(8,128)} %agg_ref.1) | copy-start | bytes 49156
  2.1 0.7 %copy-start.2 = (f32[1,1,1,8,128]{4,3,2,1,0:T(8,128)S(1)}, f32[1,1,1,8,128]{4,3,2,1,0:T(8,128)}, u32[]{:S(2)}) copy-start(f32[1,1,1,8,128]{4,3,2,1,0:T(8,128)} %current_ref.1) | copy-start | bytes 12292
  2.8 0.7 %copy-start.3 = (s32[1,1,1,8,128]{4,3,2,1,0:T(8,128)S(1)}, s32[1,1,1,8,128]{4,3,2,1,0:T(8,128)}, u32[]{:S(2)}) copy-start(s32[1,1,1,8,128]{4,3,2,1,0:T(8,128)} %node_ref.1) | copy-start | bytes 12292
  3.4 0.7 %copy-start.4 = (s32[1,1,1,8]{3,2,1,0:T(1,128)S(1)}, s32[1,1,1,8]{3,2,1,0:T(1,128)}, u32[]{:S(2)}) copy-start(s32[1,1,1,8]{3,2,1,0:T(1,128)} %count_ref.1) | copy-start | bytes 100

commit v2 on v1

--- a/solution.py
+++ b/solution.py
@@ -25,7 +25,7 @@
 
 
 def each(count, step):
-    if count <= 8:
+    if count <= 32:
         for k in range(1, count):
             step(k)
     else:
@@ -46,11 +46,12 @@
 
 def kernel(
     dims,
-    shunt_ref, agg_ref, current_ref, node_ref, count_ref,
-    voltage_ref, residual_ref,
+    shunt_in, agg_in, current_in, node_in, count_in,
+    result_ref,
+    shunt_ref, agg_ref, current_ref, node_ref, count_ref, input_s,
     msg, box, row_hot, col_hot, coarse_out, coarse_in, field_out, field_in,
-    part_out, part_tile, part_layer,
-    msg_s, msg_r, coarse_s, coarse_r, field_s, field_r, tile_s, tile_r, layer_s, layer_r,
+    part_out, part_in,
+    msg_s, msg_r, coarse_s, coarse_r, field_s, field_r, part_s, part_r,
 ):
     layers, n_tx, n_ty = dims
     tiles = n_tx * n_ty
@@ -63,8 +64,21 @@
     def tile_device(d):
         return {"layer": lay, "tx": d // n_ty, "ty": lax.rem(d, n_ty)}
 
-    def layer_device(l):
-        return {"layer": l, "tx": tx, "ty": ty}
+    everyone = layers * tiles
+    place = lay * tiles + me
+
+    def any_device(d):
+        rest = lax.rem(d, tiles)
+        return {"layer": d // tiles, "tx": rest // n_ty, "ty": lax.rem(rest, n_ty)}
+
+    loads = [
+        pltpu.make_async_copy(source, target, input_s.at[k])
+        for k, (source, target) in enumerate((
+            (count_in, count_ref), (current_in, current_ref), (node_in, node_ref),
+            (agg_in, agg_ref), (shunt_in, shunt_ref)))
+    ]
+    for load in loads:
+        load.start()
 
     def beside_layer(da, dx, dy):
         here = True
@@ -76,10 +90,8 @@
         return here
 
     barrier = pltpu.get_barrier_semaphore()
-    each(tiles, lambda k: pl.semaphore_signal(
-        barrier, inc=1, device_id=tile_device(lax.rem(me + k, tiles)), device_id_type=MESH))
-    each(layers, lambda k: pl.semaphore_signal(
-        barrier, inc=1, device_id=layer_device(lax.rem(lay + k, layers)), device_id_type=MESH))
+    each(everyone, lambda k: pl.semaphore_signal(
+        barrier, inc=1, device_id=any_device(lax.rem(place + k, everyone)), device_id_type=MESH))
 
     for k, (a, b) in enumerate(AROUND):
         if (a, b) != (0, 0):
@@ -91,6 +103,8 @@
         def _(k=k):
             field_in[:, k] = jnp.zeros((ITERS,) + field_in.shape[2:], jnp.float32)
 
+    for load in loads[:3]:
+        load.wait()
     square = (tiles, tiles)
     counts = jnp.broadcast_to(count_ref[0, 0].astype(jnp.float32), square)
     counts = jnp.sum(
@@ -99,23 +113,8 @@
     msg[:, 0, :] = jnp.where(iota(slots, 1).astype(jnp.float32) < counts, current_ref[0, 0, 0], 0.0)
     msg[:, 1, :] = node_ref[0, 0, 0].astype(jnp.float32)
 
-    pl.semaphore_wait(barrier, tiles + layers - 2)
-
-    def slot_copy(k):
-        return pltpu.make_async_remote_copy(
-            src_ref=msg.at[lax.rem(me + k, tiles)], dst_ref=box.at[me],
-            send_sem=msg_s.at[k], recv_sem=msg_r.at[k],
-            device_id=tile_device(lax.rem(me + k, tiles)), device_id_type=MESH)
-
-    def slot_arrival(k):
-        return pltpu.make_async_remote_copy(
-            src_ref=msg.at[me], dst_ref=box.at[lax.rem(me + tiles - k, tiles)],
-            send_sem=msg_s.at[k], recv_sem=msg_r.at[k],
-            device_id=tile_device(lax.rem(me + k, tiles)), device_id_type=MESH)
-
-    each(tiles, lambda k: slot_copy(k).start())
-    box[me] = msg[me]
-
+    for load in loads[3:]:
+        load.wait()
     agg = agg_ref[0]
     agg_p = agg // CGY
     agg_q = agg % CGY
@@ -220,10 +219,27 @@
     diagonal = shunt + (4.0 + 2.0 * VIA_CONDUCTANCE)
     own_diag = 4.0 * COARSE_EDGE + restrict(shunt + 2.0 * VIA_CONDUCTANCE)
     coarse_out[ITERS] = own_diag
+    inverse = 1.0 / diagonal
+
+    pl.semaphore_wait(barrier, everyone - 1)
+
+    def slot_copy(k):
+        return pltpu.make_async_remote_copy(
+            src_ref=msg.at[lax.rem(me + k, tiles)], dst_ref=box.at[me],
+            send_sem=msg_s, recv_sem=msg_r,
+            device_id=tile_device(lax.rem(me + k, tiles)), device_id_type=MESH)
+
+    def slot_all():
+        return pltpu.make_async_remote_copy(
+            src_ref=msg.at[pl.ds(0, tiles - 1)], dst_ref=box.at[pl.ds(0, tiles - 1)],
+            send_sem=msg_s, recv_sem=msg_r,
+            device_id=tile_device(lax.rem(me + 1, tiles)), device_id_type=MESH)
+
+    each(tiles, lambda k: slot_copy(k).start())
+    box[me] = msg[me]
     coarse_each(lambda k: coarse_copy(ITERS, k).start())
-    inverse = 1.0 / diagonal
-
-    each(tiles, lambda k: slot_arrival(k).wait_recv())
+
+    slot_all().wait_recv()
 
     def scatter(first):
         lefts, rights = [], []
@@ -264,10 +280,14 @@
         coarse_each(lambda k: coarse_copy(turn, k).start())
         local = power * inverse
         if turn == 0:
+            slot_all().wait_send()
+            coarse_each(lambda k: coarse_copy(ITERS, k).wait_send())
             coarse_each(lambda k: coarse_arrival(ITERS, k).wait_recv())
             coarse_diag = coarse_block(ITERS, own_diag)
             coarse_inverse = jnp.where(
                 coarse_diag > 0.0, RELAXATION / jnp.maximum(coarse_diag, 1.0), 0.0)
+        else:
+            field_each(lambda k: field_copy(turn - 1, k).wait_send())
         coarse_each(lambda k: coarse_arrival(turn, k).wait_recv())
         rhs = coarse_block(turn, own)
         potential = rhs * coarse_inverse
@@ -288,6 +308,8 @@
              for i in range(height // 8)], axis=0)
         field_out[turn] = smooth
         field_each(lambda k: field_copy(turn, k).start())
+        if turn + 1 < ITERS:
+            coarse_each(lambda k: coarse_copy(turn, k).wait_send())
         field_each(lambda k: field_arrival(turn, k).wait_recv())
         north = jnp.where(
             big_row == 0, field_in[turn, 2, height - 1:height, :], pltpu.roll(smooth, 1, 0))
@@ -303,43 +325,33 @@
         powers.append(power)
         smooths.append(smooth)
 
-    for k in range(2 * ITERS):
-        product = powers[(k + 1) // 2] * smooths[k // 2]
-        part_out[0, k:k + 1, :] = jnp.sum(product, axis=0, keepdims=True)
-    part_out[0, 6:8, :] = jnp.zeros((2, breadth), jnp.float32)
-
-    def tile_copy(k):
-        return pltpu.make_async_remote_copy(
-            src_ref=part_out.at[0], dst_ref=part_tile.at[me],
-            send_sem=tile_s.at[k], recv_sem=tile_r.at[k],
-            device_id=tile_device(lax.rem(me + k, tiles)), device_id_type=MESH)
-
-    def tile_arrival(k):
-        return pltpu.make_async_remote_copy(
-            src_ref=part_out.at[0], dst_ref=part_tile.at[lax.rem(me + tiles - k, tiles)],
-            send_sem=tile_s.at[k], recv_sem=tile_r.at[k],
-            device_id=tile_device(lax.rem(me + k, tiles)), device_id_type=MESH)
-
-    def layer_copy(k):
-        return pltpu.make_async_remote_copy(
-            src_ref=part_out.at[1], dst_ref=part_layer.at[lay],
-            send_sem=layer_s.at[k], recv_sem=layer_r.at[k],
-            device_id=layer_device(lax.rem(lay + k, layers)), device_id_type=MESH)
-
-    def layer_arrival(k):
-        return pltpu.make_async_remote_copy(
-            src_ref=part_out.at[1], dst_ref=part_layer.at[lax.rem(lay + layers - k, layers)],
-            send_sem=layer_s.at[k], recv_sem=layer_r.at[k],
-            device_id=layer_device(lax.rem(lay + k, layers)), device_id_type=MESH)
-
-    each(tiles, lambda k: tile_copy(k).start())
-    part_tile[me] = part_out[0]
-    each(tiles, lambda k: tile_arrival(k).wait_recv())
-    part_out[1] = jnp.sum(part_tile[...], axis=0)
-    each(layers, lambda k: layer_copy(k).start())
-    part_layer[lay] = part_out[1]
-    each(layers, lambda k: layer_arrival(k).wait_recv())
-    sums = jnp.sum(jnp.sum(part_layer[...], axis=0), axis=1, keepdims=True)
+    sums = [
+        jnp.sum(powers[(k + 1) // 2] * smooths[k // 2], axis=0, keepdims=True)
+        for k in range(2 * ITERS)
+    ]
+    sums.append(jnp.zeros((8 - 2 * ITERS, breadth), jnp.float32))
+    sums = jnp.sum(jnp.concatenate(sums, axis=0), axis=1, keepdims=True)
+    spot = iota((8, breadth), 0) == lane
+    part_out[...] = jnp.sum(jnp.where(spot, sums, 0.0), axis=0, keepdims=True)
+
+    def part_copy(k):
+        return pltpu.make_async_remote_copy(
+            src_ref=part_out, dst_ref=part_in.at[place], send_sem=part_s, recv_sem=part_r,
+            device_id=any_device(lax.rem(place + k, everyone)), device_id_type=MESH)
+
+    def part_all():
+        rows = part_in.at[pl.ds(0, everyone - 1)]
+        return pltpu.make_async_remote_copy(
+            src_ref=rows, dst_ref=rows, send_sem=part_s, recv_sem=part_r,
+            device_id=any_device(lax.rem(place + 1, everyone)), device_id_type=MESH)
+
+    each(everyone, lambda k: part_copy(k).start())
+    part_in[place] = part_out[...]
+    coarse_each(lambda k: coarse_copy(ITERS - 1, k).wait_send())
+    field_each(lambda k: field_copy(ITERS - 1, k).wait_send())
+    part_all().wait_recv()
+    sums = jnp.sum(part_in[...], axis=0)
+    sums = jnp.sum(jnp.where(spot, sums, 0.0), axis=1, keepdims=True)
     moments = [sums[k:k + 1, :] for k in range(2 * ITERS)]
     energies = [moments[k + 1] + SHIFT * moments[k] for k in range(2 * ITERS - 1)]
 
@@ -364,16 +376,9 @@
         voltage = voltage + volt[i] * smooths[i]
     for i in range(1, ITERS + 1):
         residual = residual + res[i] * powers[i]
-    voltage_ref[0] = voltage
-    residual_ref[0] = residual
-
-    each(tiles, lambda k: slot_copy(k).wait_send())
-    for turn in range(ITERS + 1):
-        coarse_each(lambda k: coarse_copy(turn, k).wait_send())
-    for turn in range(ITERS):
-        field_each(lambda k: field_copy(turn, k).wait_send())
-    each(tiles, lambda k: tile_copy(k).wait_send())
-    each(layers, lambda k: layer_copy(k).wait_send())
+    result_ref[0] = voltage
+    result_ref[1] = residual
+    part_all().wait_send()
 
 
 def solution(mesh):
@@ -385,12 +390,14 @@
         f32 = jnp.float32
         dma = pltpu.SemaphoreType.DMA
         vmem = pl.BlockSpec(memory_space=pltpu.VMEM)
-        return tuple(pl.pallas_call(
+        out = pl.pallas_call(
             functools.partial(kernel, (layers, n_tx, n_ty)),
-            out_shape=[jax.ShapeDtypeStruct(shunt.shape, f32)] * 2,
-            in_specs=[vmem] * 5,
-            out_specs=[vmem] * 2,
+            out_shape=jax.ShapeDtypeStruct((2,) + shunt.shape[1:], f32),
+            in_specs=[pl.BlockSpec(memory_space=pltpu.HBM)] * 5,
+            out_specs=vmem,
             scratch_shapes=[
+                *(pltpu.VMEM(x.shape, x.dtype) for x in (shunt, agg, current, node, count)),
+                dma((5,)),
                 pltpu.VMEM((tiles, 2, current.shape[4]), f32),
                 pltpu.VMEM((tiles, 2, current.shape[4]), f32),
                 pltpu.VMEM((height, CGX, breadth), f32),
@@ -399,18 +406,17 @@
                 pltpu.VMEM((ITERS + 1, 9, CGX, breadth), f32),
                 pltpu.VMEM((ITERS, height, breadth), f32),
                 pltpu.VMEM((ITERS, 6, height, breadth), f32),
-                pltpu.VMEM((2, 8, breadth), f32),
-                pltpu.VMEM((tiles, 8, breadth), f32),
-                pltpu.VMEM((layers, 8, breadth), f32),
-                dma((tiles,)), dma((tiles,)),
+                pltpu.VMEM((1, breadth), f32),
+                pltpu.VMEM((layers * tiles, 1, breadth), f32),
+                dma, dma,
                 dma((ITERS + 1, 9)), dma((ITERS + 1, 9)),
                 dma((ITERS, 6)), dma((ITERS, 6)),
-                dma((tiles,)), dma((tiles,)),
-                dma((layers,)), dma((layers,)),
+                dma, dma,
             ],
             compiler_params=pltpu.CompilerParams(
-                collective_id=0, has_side_effects=True, vmem_limit_bytes=32 * 1024 * 1024),
-        )(shunt, agg, current, node, count))
+                collective_id=0, has_side_effects=True, vmem_limit_bytes=60 * 1024 * 1024),
+        )(shunt, agg, current, node, count)
+        return out[0:1], out[1:2]
 
     in_specs = (
         P("layer", "tx", "ty"),

time: 43 us -> 38.9 us (0.905)
  local copies, waits for them, and re-layouts: 4.67 us -> 1.35 us
  Pallas kernels: 37.3 us -> 36.6 us
    unnamed x12 -> x0, local copies, waits for them, and re-layouts: 4.67 us -> none
    slice x0 -> x1, local copies, waits for them, and re-layouts: none -> 1.35 us  [body(): return (out[0:1], out[1:2])]
    pallas_call x1, Pallas kernels: 37.3 us -> 36.6 us  [body(): pl.pallas_call(functools.partial(kernel, (layers, n_tx, n_ty)), out_shape...]
where the time goes in v2:
time: 38.9 us; the launch traced here: 38.6 us
  Pallas kernels  36.6 us (94%)
  local copies, waits for them, and re-layouts  1.35 us (3%)
  between operations  0.64 us (2%)
    pallas_call x1, Pallas kernels, body(): pl.pallas_call(functools.partial(kernel, (layers, n_tx, n_ty)), out_shape...  36.6 us
    slice x1, local copies, waits for them, and re-layouts, body(): return (out[0:1], out[1:2])  1.35 us

profile of v2, /device:TPU:0, one launch (start us, length us, event | category | flops | bytes accessed | tf_op | source)
XLA Modules:
  0.0 38.6 jit_solution(4685924014379863206)
XLA Ops:
  0.6 36.6 %shard_map.68 = f32[2,32,128]{2,1,0:T(8,128)} custom-call(f32[1,32,128]{2,1,0:T(8,128)} %shunt_in.1, s32[1,32,128]{2,1,0:T(8,128)} %agg_in.1, f32[1,1,1,8,128]{4,3,2,1,0:T(8,128)} %current_in.1, s32[1,1,1,8,128]{4,3,2,1,0:T(8,128)} %node_in.1, s32[1,1,1,8]{3,2,1,0:T(1,128)} %count_in.1), custom_call_target="tpu_custom_call" | custom-call | tf_op jit(solution)/shard_map/pallas_call | solution.py:393
  37.3 1.3 %fusion = (f32[1,32,128]{2,1,0:T(8,128)}, f32[1,32,128]{2,1,0:T(8,128)}) fusion(f32[2,32,128]{2,1,0:T(8,128)} %shard_map.68), kind=kLoop, calls=%fused_computation | loop fusion | bytes 65536 | tf_op jit(solution)/shard_map/slice | solution.py:419

commit v3 on v2

--- a/solution.py
+++ b/solution.py
@@ -16,7 +16,6 @@
 RELAXATION = 0.6
 SHIFT = 1.25
 MESH = pl.DeviceIdType.MESH
-AROUND = [(a, b) for a in (-1, 0, 1) for b in (-1, 0, 1)]
 SIDES = [(-1, 0, 0), (1, 0, 0), (0, -1, 0), (0, 1, 0), (0, 0, -1), (0, 0, 1)]
 
 
@@ -36,6 +35,13 @@
         lax.fori_loop(1, count, run, 0)
 
 
+def coarse_places(n_tx, n_ty):
+    own = [(0, a, b) for a in range(-2, 3) for b in range(-2, 3)
+           if (a, b) != (0, 0) and abs(a) + abs(b) < 4]
+    other = [(d, a, b) for d in (-1, 1) for a in (-1, 0, 1) for b in (-1, 0, 1)]
+    return [p for p in own + other if abs(p[1]) < n_tx and abs(p[2]) < n_ty]
+
+
 def quadratic(moments, coefs):
     total = 0.0
     for i, a in enumerate(coefs):
@@ -49,9 +55,9 @@
     shunt_in, agg_in, current_in, node_in, count_in,
     result_ref,
     shunt_ref, agg_ref, current_ref, node_ref, count_ref, input_s,
-    msg, box, row_hot, col_hot, coarse_out, coarse_in, field_out, field_in,
+    msg, box, agg_side, row_hot, col_hot, coarse_out, coarse_in, field_out, field_in,
     part_out, part_in,
-    msg_s, msg_r, coarse_s, coarse_r, field_s, field_r, part_s, part_r,
+    msg_s, msg_r, side_s, side_r, coarse_s, coarse_r, field_s, field_r, part_s, part_r,
 ):
     layers, n_tx, n_ty = dims
     tiles = n_tx * n_ty
@@ -60,6 +66,7 @@
     tx = lax.axis_index("tx")
     ty = lax.axis_index("ty")
     me = tx * n_ty + ty
+    places = coarse_places(n_tx, n_ty)
 
     def tile_device(d):
         return {"layer": lay, "tx": d // n_ty, "ty": lax.rem(d, n_ty)}
@@ -84,24 +91,24 @@
         here = True
         for value, delta, size in ((lay, da, layers), (tx, dx, n_tx), (ty, dy, n_ty)):
             if delta < 0:
-                here = jnp.logical_and(here, value > 0)
+                here = jnp.logical_and(here, value >= -delta)
             if delta > 0:
-                here = jnp.logical_and(here, value < size - 1)
+                here = jnp.logical_and(here, value < size - delta)
         return here
 
     barrier = pltpu.get_barrier_semaphore()
     each(everyone, lambda k: pl.semaphore_signal(
         barrier, inc=1, device_id=any_device(lax.rem(place + k, everyone)), device_id_type=MESH))
 
-    for k, (a, b) in enumerate(AROUND):
-        if (a, b) != (0, 0):
-            @pl.when(jnp.logical_not(beside_layer(0, a, b)))
-            def _(k=k):
-                coarse_in[:, k] = jnp.zeros((ITERS + 1,) + coarse_in.shape[2:], jnp.float32)
+    for k, offset in enumerate(places):
+        @pl.when(jnp.logical_not(beside_layer(*offset)))
+        def _(k=k):
+            coarse_in[:, k] = jnp.zeros((ITERS + 1, 1, breadth), jnp.float32)
     for k, side in enumerate(SIDES):
         @pl.when(jnp.logical_not(beside_layer(*side)))
         def _(k=k):
-            field_in[:, k] = jnp.zeros((ITERS,) + field_in.shape[2:], jnp.float32)
+            field_in[:, k] = jnp.zeros((ITERS, height, breadth), jnp.float32)
+            agg_side[k] = jnp.zeros((height, breadth), jnp.int32)
 
     for load in loads[:3]:
         load.wait()
@@ -155,36 +162,67 @@
             total = total + pltpu.roll(total, shift, 1)
         return total
 
+    cell = CGY * iota((CGX, breadth), 0) + lane % CGY
+
+    def flatten(block):
+        block = jnp.where(group == iota((CGX, breadth), 0), block, 0.0)
+        return jnp.sum(block, axis=0, keepdims=True)
+
+    def pick(row, index):
+        row = jnp.broadcast_to(row, (CGX, breadth))
+        return jnp.take_along_axis(row, index, axis=1, mode="promise_in_bounds")
+
     def coarse_copy(turn, k):
-        a, b = AROUND[k]
-        return pltpu.make_async_remote_copy(
-            src_ref=coarse_out.at[turn], dst_ref=coarse_in.at[turn, 8 - k],
-            send_sem=coarse_s.at[turn, k], recv_sem=coarse_r.at[turn, 8 - k],
-            device_id={"layer": lay, "tx": tx + a, "ty": ty + b}, device_id_type=MESH)
+        da, dx, dy = places[k]
+        there = places.index((-da, -dx, -dy))
+        return pltpu.make_async_remote_copy(
+            src_ref=coarse_out.at[turn], dst_ref=coarse_in.at[turn, there],
+            send_sem=coarse_s.at[turn, k], recv_sem=coarse_r.at[turn, there],
+            device_id={"layer": lay + da, "tx": tx + dx, "ty": ty + dy}, device_id_type=MESH)
 
     def coarse_arrival(turn, k):
-        a, b = AROUND[k]
+        da, dx, dy = places[k]
         return pltpu.make_async_remote_copy(
             src_ref=coarse_out.at[turn], dst_ref=coarse_in.at[turn, k],
             send_sem=coarse_s.at[turn, k], recv_sem=coarse_r.at[turn, k],
-            device_id={"layer": lay, "tx": tx + a, "ty": ty + b}, device_id_type=MESH)
+            device_id={"layer": lay + da, "tx": tx + dx, "ty": ty + dy}, device_id_type=MESH)
 
     def coarse_each(step):
-        for k, (a, b) in enumerate(AROUND):
-            if (a, b) != (0, 0):
-                @pl.when(beside_layer(0, a, b))
-                def _(k=k):
-                    step(k)
-
-    def coarse_block(turn, own):
-        rows = []
-        for a in range(3):
-            west = coarse_in[turn, 3 * a]
-            mid = own if a == 1 else coarse_in[turn, 3 * a + 1]
-            east = coarse_in[turn, 3 * a + 2]
-            row = jnp.where(group == 0, west, jnp.where(group == 1, mid, east))
-            rows.append(jnp.where(group < 3, row, 0.0))
-        return jnp.concatenate(rows, axis=0)
+        for k, offset in enumerate(places):
+            @pl.when(beside_layer(*offset))
+            def _(k=k):
+                step(k)
+
+    reach = min(2, n_tx - 1)
+
+    def coarse_blocks(turn, own):
+        zero = jnp.zeros((CGX, breadth), jnp.float32)
+
+        def tile(offset):
+            if offset == (0, 0, 0):
+                return own
+            if offset not in places:
+                return zero
+            return pick(coarse_in[turn, places.index(offset)], cell)
+
+        def line(offsets):
+            row = zero
+            for g, offset in enumerate(offsets):
+                row = jnp.where(group == g, tile(offset), row)
+            return row
+
+        same = [line([(0, a, b) for b in range(-2, 3)]) for a in range(-reach, reach + 1)]
+        other = [line([(d, a, b) for d in (-1, 1) for b in (-1, 0, 1)]) for a in (-1, 0, 1)]
+        return jnp.concatenate(same, axis=0), jnp.concatenate(other, axis=0)
+
+    def sweeps(rhs, diag, inv):
+        potential = rhs * inv
+        for sweep in range(SWEEPS - 1):
+            beside = (
+                pltpu.roll(potential, 1, 1) + pltpu.roll(potential, breadth - 1, 1)
+                + pltpu.roll(potential, 1, 0) + pltpu.roll(potential, rhs.shape[0] - 1, 0))
+            potential = potential + inv * (rhs - (diag * potential - COARSE_EDGE * beside))
+        return potential
 
     def side_part(k, ref):
         if k == 2:
@@ -209,6 +247,20 @@
             send_sem=field_s.at[turn, k], recv_sem=field_r.at[turn, k],
             device_id={"layer": lay + da, "tx": tx + dx, "ty": ty + dy}, device_id_type=MESH)
 
+    def side_copy(k):
+        da, dx, dy = SIDES[k]
+        return pltpu.make_async_remote_copy(
+            src_ref=side_part(k, agg_ref.at[0]), dst_ref=side_part(k, agg_side.at[k ^ 1]),
+            send_sem=side_s.at[k], recv_sem=side_r.at[k ^ 1],
+            device_id={"layer": lay + da, "tx": tx + dx, "ty": ty + dy}, device_id_type=MESH)
+
+    def side_arrival(k):
+        da, dx, dy = SIDES[k]
+        return pltpu.make_async_remote_copy(
+            src_ref=side_part(k ^ 1, agg_ref.at[0]), dst_ref=side_part(k ^ 1, agg_side.at[k]),
+            send_sem=side_s.at[k], recv_sem=side_r.at[k],
+            device_id={"layer": lay + da, "tx": tx + dx, "ty": ty + dy}, device_id_type=MESH)
+
     def field_each(step):
         for k, side in enumerate(SIDES):
             @pl.when(beside_layer(*side))
@@ -218,7 +270,7 @@
     shunt = shunt_ref[0]
     diagonal = shunt + (4.0 + 2.0 * VIA_CONDUCTANCE)
     own_diag = 4.0 * COARSE_EDGE + restrict(shunt + 2.0 * VIA_CONDUCTANCE)
-    coarse_out[ITERS] = own_diag
+    coarse_out[ITERS] = flatten(own_diag)
     inverse = 1.0 / diagonal
 
     pl.semaphore_wait(barrier, everyone - 1)
@@ -237,6 +289,7 @@
 
     each(tiles, lambda k: slot_copy(k).start())
     box[me] = msg[me]
+    field_each(lambda k: side_copy(k).start())
     coarse_each(lambda k: coarse_copy(ITERS, k).start())
 
     slot_all().wait_recv()
@@ -275,52 +328,54 @@
     power = sources
     powers, smooths = [sources], []
     for turn in range(ITERS):
+        local = power * inverse
+        field_out[turn] = local
+        field_each(lambda k: field_copy(turn, k).start())
         own = restrict(power)
-        coarse_out[turn] = own
+        coarse_out[turn] = flatten(own)
         coarse_each(lambda k: coarse_copy(turn, k).start())
-        local = power * inverse
         if turn == 0:
             slot_all().wait_send()
             coarse_each(lambda k: coarse_copy(ITERS, k).wait_send())
             coarse_each(lambda k: coarse_arrival(ITERS, k).wait_recv())
-            coarse_diag = coarse_block(ITERS, own_diag)
-            coarse_inverse = jnp.where(
-                coarse_diag > 0.0, RELAXATION / jnp.maximum(coarse_diag, 1.0), 0.0)
+            field_each(lambda k: side_copy(k).wait_send())
+            field_each(lambda k: side_arrival(k).wait_recv())
+            coarse_diag = coarse_blocks(ITERS, own_diag)
+            coarse_inverse = [
+                jnp.where(d > 0.0, RELAXATION / jnp.maximum(d, 1.0), 0.0) for d in coarse_diag]
         else:
             field_each(lambda k: field_copy(turn - 1, k).wait_send())
+            coarse_each(lambda k: coarse_copy(turn - 1, k).wait_send())
+        field_each(lambda k: field_arrival(turn, k).wait_recv())
         coarse_each(lambda k: coarse_arrival(turn, k).wait_recv())
-        rhs = coarse_block(turn, own)
-        potential = rhs * coarse_inverse
-        for sweep in range(SWEEPS - 1):
-            beside = (
-                pltpu.roll(potential, 1, 1) + pltpu.roll(potential, breadth - 1, 1)
-                + pltpu.roll(potential, 1, 0) + pltpu.roll(potential, 3 * CGX - 1, 0))
-            potential = potential + coarse_inverse * (
-                rhs - (coarse_diag * potential - COARSE_EDGE * beside))
-        table = jnp.where(group == 1, potential[CGX:2 * CGX], 0.0)
-        for shift in (16, 32, 64):
-            table = table + pltpu.roll(table, shift, 1)
-        table = jnp.where(group == iota((CGX, breadth), 0), table, 0.0)
-        for shift in (4, 2, 1):
-            table = table + pltpu.roll(table, shift, 0)
-        smooth = local + jnp.concatenate(
-            [jnp.take_along_axis(table, agg[8 * i:8 * i + 8], axis=1, mode="promise_in_bounds")
-             for i in range(height // 8)], axis=0)
-        field_out[turn] = smooth
-        field_each(lambda k: field_copy(turn, k).start())
-        if turn + 1 < ITERS:
-            coarse_each(lambda k: coarse_copy(turn, k).wait_send())
-        field_each(lambda k: field_arrival(turn, k).wait_recv())
-        north = jnp.where(
-            big_row == 0, field_in[turn, 2, height - 1:height, :], pltpu.roll(smooth, 1, 0))
-        south = jnp.where(
-            big_row == height - 1, field_in[turn, 3, 0:1, :], pltpu.roll(smooth, height - 1, 0))
-        west = pltpu.roll(
-            jnp.where(big_lane == breadth - 1, field_in[turn, 4], smooth), 1, 1)
-        east = pltpu.roll(
-            jnp.where(big_lane == 0, field_in[turn, 5], smooth), breadth - 1, 1)
+        same, other = [
+            sweeps(*x) for x in zip(coarse_blocks(turn, own), coarse_diag, coarse_inverse)]
+
+        def table(block, row, g):
+            part = block[CGX * row:CGX * (row + 1)]
+            part = jnp.take_along_axis(
+                part, CGY * g + lane % CGY, axis=1, mode="promise_in_bounds")
+            return flatten(part)
+
+        def spread(row, labels):
+            return jnp.concatenate(
+                [pick(row, labels[8 * i:8 * i + 8]) for i in range(labels.shape[0] // 8)], axis=0)
+
+        smooth = local + spread(table(same, reach, 2), agg)
+        below = field_in[turn, 0] + spread(table(other, 1, 1), agg_side[0])
+        above = field_in[turn, 1] + spread(table(other, 1, 4), agg_side[1])
+        west = field_in[turn, 4] + spread(table(same, reach, 1), agg_side[4])
+        east = field_in[turn, 5] + spread(table(same, reach, 3), agg_side[5])
+        north = field_in[turn, 2, height - 8:height, :] + pick(
+            table(same, reach - 1, 2), agg_side[2, height - 8:height, :])
+        south = field_in[turn, 3, 0:8, :] + pick(
+            table(same, reach + 1, 2), agg_side[3, 0:8, :])
+        north = jnp.where(big_row == 0, north[7:8, :], pltpu.roll(smooth, 1, 0))
+        south = jnp.where(big_row == height - 1, south[0:1, :], pltpu.roll(smooth, height - 1, 0))
+        west = pltpu.roll(jnp.where(big_lane == breadth - 1, west, smooth), 1, 1)
+        east = pltpu.roll(jnp.where(big_lane == 0, east, smooth), breadth - 1, 1)
         image = (diagonal * smooth - (north + south + west + east)
-                 - VIA_CONDUCTANCE * (field_in[turn, 0] + field_in[turn, 1]))
+                 - VIA_CONDUCTANCE * (below + above))
         power = image - SHIFT * power
         powers.append(power)
         smooths.append(smooth)
@@ -387,6 +442,7 @@
 
     def body(shunt, agg, current, node, count):
         height, breadth = shunt.shape[1], shunt.shape[2]
+        near = len(coarse_places(n_tx, n_ty))
         f32 = jnp.float32
         dma = pltpu.SemaphoreType.DMA
         vmem = pl.BlockSpec(memory_space=pltpu.VMEM)
@@ -400,16 +456,18 @@
                 dma((5,)),
                 pltpu.VMEM((tiles, 2, current.shape[4]), f32),
                 pltpu.VMEM((tiles, 2, current.shape[4]), f32),
+                pltpu.VMEM((6, height, breadth), jnp.int32),
                 pltpu.VMEM((height, CGX, breadth), f32),
                 pltpu.VMEM((CGY * height // 2, 2 * breadth), jnp.bfloat16),
-                pltpu.VMEM((ITERS + 1, CGX, breadth), f32),
-                pltpu.VMEM((ITERS + 1, 9, CGX, breadth), f32),
+                pltpu.VMEM((ITERS + 1, 1, breadth), f32),
+                pltpu.VMEM((ITERS + 1, near, 1, breadth), f32),
                 pltpu.VMEM((ITERS, height, breadth), f32),
                 pltpu.VMEM((ITERS, 6, height, breadth), f32),
                 pltpu.VMEM((1, breadth), f32),
                 pltpu.VMEM((layers * tiles, 1, breadth), f32),
                 dma, dma,
-                dma((ITERS + 1, 9)), dma((ITERS + 1, 9)),
+                dma((6,)), dma((6,)),
+                dma((ITERS + 1, near)), dma((ITERS + 1, near)),
                 dma((ITERS, 6)), dma((ITERS, 6)),
                 dma, dma,
             ],

time: 38.9 us -> 33.5 us (0.86)
  Pallas kernels: 36.6 us -> 31.3 us
    pallas_call x1, Pallas kernels: 36.6 us -> 31.3 us  [body(): pl.pallas_call(functools.partial(kernel, (layers, n_tx, n_ty)), out_shape...]
where the time goes in v3:
time: 33.5 us; the launch traced here: 33.3 us
  Pallas kernels  31.3 us (93%)
  local copies, waits for them, and re-layouts  1.35 us (4%)
  between operations  0.64 us (2%)
    pallas_call x1, Pallas kernels, body(): pl.pallas_call(functools.partial(kernel, (layers, n_tx, n_ty)), out_shape...  31.3 us
    slice x1, local copies, waits for them, and re-layouts, body(): return (out[0:1], out[1:2])  1.35 us

profile of v3, /device:TPU:0, one launch (start us, length us, event | category | flops | bytes accessed | tf_op | source)
XLA Modules:
  0.0 33.3 jit_solution(12322666829226808021)
XLA Ops:
  0.6 31.3 %shard_map.68 = f32[2,32,128]{2,1,0:T(8,128)} custom-call(f32[1,32,128]{2,1,0:T(8,128)} %shunt_in.1, s32[1,32,128]{2,1,0:T(8,128)} %agg_in.1, f32[1,1,1,8,128]{4,3,2,1,0:T(8,128)} %current_in.1, s32[1,1,1,8,128]{4,3,2,1,0:T(8,128)} %node_in.1, s32[1,1,1,8]{3,2,1,0:T(1,128)} %count_in.1), custom_call_target="tpu_custom_call" | custom-call | tf_op jit(solution)/shard_map/pallas_call | solution.py:449
  32.0 1.3 %fusion = (f32[1,32,128]{2,1,0:T(8,128)}, f32[1,32,128]{2,1,0:T(8,128)}) fusion(f32[2,32,128]{2,1,0:T(8,128)} %shard_map.68), kind=kLoop, calls=%fused_computation | loop fusion | bytes 65536 | tf_op jit(solution)/shard_map/slice | solution.py:477
